TPU v7x, 32 devices: a whole 2x2x4 slice. The times are simulated.
32 devices in a mesh: dp: 8 (over z, core), fsdp: 4 (over y, x).
Axes of the slice: x: 2, y: 2, z: 4, core: 2. Of those that a mesh axis runs over, the one named last changes fastest.
Arguments:
- inputs: bfloat16 [8, 1152, 2048], P('dp', 'fsdp'), may hold values from -6 to 6
- modality: int32 [8, 1152], P('dp', 'fsdp'), may hold values from 0 to 2, as said below
- gain: bfloat16 [2048], P(('dp', 'fsdp')), may hold values from 0.5 to 1.5
- in_weight: bfloat16 [3, 2048, 8192], P(None, None, ('dp', 'fsdp')), may hold values from -0.125 to 0.125
- conv_weight: bfloat16 [4, 4096], P(None, ('dp', 'fsdp')), may hold values from -0.5 to 0.5
- conv_bias: bfloat16 [4096], P(('dp', 'fsdp')), may hold values from -0.5 to 0.5
- x_weight: bfloat16 [3, 4096, 160], P(None, ('dp', 'fsdp')), may hold values from -0.09375 to 0.09375
- dt_weight: bfloat16 [3, 128, 4096], P(None, None, ('dp', 'fsdp')), may hold values from -0.5 to 0.5
- dt_bias: bfloat16 [3, 4096], P(None, ('dp', 'fsdp')), may hold values from -5.5 to -3.5
- log_rate: bfloat16 [16, 4096], P(None, ('dp', 'fsdp')), may hold values from -3 to 1.59375
- skip_gain: bfloat16 [4096], P(('dp', 'fsdp')), may hold values from 0.5 to 1.5
- out_weight: bfloat16 [3, 4096, 2048], P(None, ('dp', 'fsdp')), may hold values from -0.25 to 0.25
- out_grad: bfloat16 [8, 1152, 2048], P('dp', 'fsdp'), may hold values from -6 to 6
Outputs:
- output: bfloat16 [8, 1152, 2048], P('dp', 'fsdp')
- input_grad: float32 [8, 1152, 2048], P('dp', 'fsdp')
- gain_grad: float32 [2048], P(('dp', 'fsdp'))
- in_weight_grad: float32 [3, 2048, 8192], P(None, None, ('dp', 'fsdp'))
- conv_weight_grad: float32 [4, 4096], P(None, ('dp', 'fsdp'))
- conv_bias_grad: float32 [4096], P(('dp', 'fsdp'))
- x_weight_grad: float32 [3, 4096, 160], P(None, ('dp', 'fsdp'))
- dt_weight_grad: float32 [3, 128, 4096], P(None, None, ('dp', 'fsdp'))
- dt_bias_grad: float32 [3, 4096], P(None, ('dp', 'fsdp'))
- log_rate_grad: float32 [16, 4096], P(None, ('dp', 'fsdp'))
- skip_gain_grad: float32 [4096], P(('dp', 'fsdp'))
- out_weight_grad: float32 [3, 4096, 2048], P(None, ('dp', 'fsdp'))
Inputs may be any that keep to these rules, and one draw needn't show every extreme that they name: The modality of each token, one of 3.
All inputs are finite; a program needn't handle non-finite values.
Results may differ from a plain program's by a relative error of at most 0.0081.
The roundings to bfloat16 on the way count: a program that leaves them out, or rounds other values in their place, can miss the bound.
Values may be sent and summed in bfloat16 or wider, within the bound.
No kernel may reach another device: no remote copies, remote signals or barrier semaphores. Data moves between devices by JAX's collectives and lax.ppermute only.
A program may use at most 640 MiB of HBM per device.

v0:
```python
import math

import jax
import jax.numpy as jnp
from jax import lax
from jax.sharding import PartitionSpec as P

epsilon = 1e-05


def passed_along(value, axis, steps):
    count = lax.axis_size(axis)
    initial, last = (max(0, -steps), min(count, count - steps))
    return lax.ppermute(value, axis, [(source, source + steps) for source in range(initial, last)])


def carried_in(array, axis, combine, identity, reverse):
    count, here = (lax.axis_size(axis), lax.axis_index(axis))
    everything = jax.tree.map(lambda part: lax.all_gather(part, axis), array)
    start = jax.tree.map(
        lambda part, zero: jnp.broadcast_to(jnp.asarray(zero, part.dtype), part.shape),
        array,
        identity,
    )

    def step(k, before):
        at = count - 1 - k if reverse else k
        reached = at > here if reverse else at < here
        new = combine(before, jax.tree.map(lambda part: part[at], everything))
        return jax.tree.map(lambda a, b: jnp.where(reached, a, b), new, before)

    return lax.fori_loop(0, count, step, start)


def time_blocks(values):
    seq_count, length, width = values.shape
    block_len = math.gcd(16, length)
    moved = jnp.swapaxes(values, 0, 1)
    return moved.reshape(length // block_len, block_len, seq_count, width)


def from_blocks(values, seq_count):
    count, block_len, _, width = values.shape
    return jnp.swapaxes(values.reshape(count * block_len, seq_count, width), 0, 1)


def advance(state, d_row, u_row, b_row, rate):
    return (
        jnp.exp(d_row[:, None, :] * rate) * state + (d_row * u_row)[:, None, :] * b_row[:, :, None]
    )


def final_state(delta, u_act, b_in, rate):

    def final_block_fn(state, block):
        d_blk, u_blk, b_blk = block
        for index in range(d_blk.shape[0]):
            state = advance(state, d_blk[index], u_blk[index], b_blk[index], rate)
        return (state, None)

    start = jnp.zeros((delta.shape[0], rate.shape[0], rate.shape[1]), jnp.float32)
    state, _ = lax.scan(
        final_block_fn, start, (time_blocks(delta), time_blocks(u_act), time_blocks(b_in))
    )
    return state


def scan_outputs(delta, u_act, b_in, c_out, rate, start):

    def scan_block_fn(state, block):
        d_blk, u_blk, b_blk, c_blk = block
        rows = []
        for index in range(d_blk.shape[0]):
            state = advance(state, d_blk[index], u_blk[index], b_blk[index], rate)
            rows.append(jnp.sum(c_blk[index][:, :, None] * state, axis=1))
        return (state, jnp.stack(rows))

    state, outs = lax.scan(
        jax.checkpoint(scan_block_fn),
        start,
        (time_blocks(delta), time_blocks(u_act), time_blocks(b_in), time_blocks(c_out)),
    )
    return (from_blocks(outs, delta.shape[0]), state)


def adjoint_state(delta, c_out, d_y, rate):

    def adjoint_block_fn(grad, block):
        d_blk, c_blk, y_blk = block
        for index in reversed(range(d_blk.shape[0])):
            grad = grad + c_blk[index][:, :, None] * y_blk[index][:, None, :]
            grad = jnp.exp(d_blk[index][:, None, :] * rate) * grad
        return (grad, None)

    start = jnp.zeros((delta.shape[0], rate.shape[0], rate.shape[1]), jnp.float32)
    grad, _ = lax.scan(
        adjoint_block_fn,
        start,
        (time_blocks(delta), time_blocks(c_out), time_blocks(d_y)),
        reverse=True,
    )
    return grad


def mixer_part(u_act, raw, b_in, c_out, z_gate, rate_log, skip_full, start):
    delta = jax.nn.softplus(raw)
    rate = -jnp.exp(rate_log)
    y_scan, state = scan_outputs(delta, u_act, b_in, c_out, rate, start)
    return ((y_scan + skip_full * u_act) * jax.nn.silu(z_gate), state)


def convolve(extended, conv_full, conv_shift):
    taps = conv_full.shape[0]
    length = extended.shape[1] - taps + 1
    total = conv_shift
    for tap in range(taps):
        total = total + conv_full[tap] * extended[:, tap : tap + length, :]
    return jax.nn.silu(total)


def rms_norm(rows, gain_full):
    mean_sq = jnp.mean(rows * rows, axis=-1, keepdims=True)
    return rows * lax.rsqrt(mean_sq + epsilon) * gain_full


def combine(earlier, later):
    return (earlier[0] * later[0], later[0] * earlier[1] + later[1])


def mode_dot(left, weight, masks):
    total = masks[:, 0:1] * jnp.dot(left, weight[0], preferred_element_type=jnp.float32)
    for copy_index in range(1, weight.shape[0]):
        total = total + masks[:, copy_index : copy_index + 1] * jnp.dot(
            left, weight[copy_index], preferred_element_type=jnp.float32
        )
    return total


def mode_dot_back(left, weight, masks):
    dims = (((1,), (1,)), ((), ()))
    total = masks[:, 0:1] * lax.dot_general(
        left, weight[0], dims, preferred_element_type=jnp.float32
    )
    for copy_index in range(1, weight.shape[0]):
        total = total + masks[:, copy_index : copy_index + 1] * lax.dot_general(
            left, weight[copy_index], dims, preferred_element_type=jnp.float32
        )
    return total


def mode_outer(left, right, masks):
    spread = left[:, None, :] * masks.astype(left.dtype)[:, :, None]
    return lax.dot_general(
        spread, right, (((0,), (0,)), ((), ())), preferred_element_type=jnp.float32
    )


def shards(
    inputs,
    modality,
    gain,
    in_weight,
    conv_weight,
    conv_bias,
    x_weight,
    dt_weight,
    dt_bias,
    log_rate,
    skip_gain,
    out_weight,
    out_grad,
):
    seq_count, seg_len, model_width = inputs.shape
    token_count = seq_count * seg_len
    copies = in_weight.shape[0]
    masks = (
        modality.reshape(token_count)[:, None] == jnp.arange(copies, dtype=jnp.int32)[None, :]
    ).astype(jnp.float32)
    masks_low = masks.astype(jnp.bfloat16)
    (
        front_full,
        select_full,
        step_full,
        gain_all,
        conv_all,
        cshift_all,
        sbias_all,
        rlog_all,
        skip_all,
    ) = (
        lax.all_gather(in_weight, ("dp", "fsdp"), axis=2, tiled=True),
        lax.all_gather(x_weight, ("dp", "fsdp"), axis=1, tiled=True),
        lax.all_gather(dt_weight, ("dp", "fsdp"), axis=2, tiled=True),
        lax.all_gather(gain, ("dp", "fsdp"), axis=0, tiled=True),
        lax.all_gather(conv_weight, ("dp", "fsdp"), axis=1, tiled=True),
        lax.all_gather(conv_bias, ("dp", "fsdp"), axis=0, tiled=True),
        lax.all_gather(dt_bias, ("dp", "fsdp"), axis=1, tiled=True),
        lax.all_gather(log_rate, ("dp", "fsdp"), axis=1, tiled=True),
        lax.all_gather(skip_gain, ("dp", "fsdp"), axis=0, tiled=True),
    )
    gain_full = gain_all.astype(jnp.float32)
    conv_full = conv_all.astype(jnp.float32)
    conv_shift = cshift_all.astype(jnp.float32)
    bias_step = sbias_all.astype(jnp.float32)
    rate_log = rlog_all.astype(jnp.float32)
    skip_full = skip_all.astype(jnp.float32)
    inner = conv_full.shape[1]
    taps = conv_full.shape[0]
    rank = step_full.shape[1]
    states = rate_log.shape[0]
    rows_float = inputs.reshape(token_count, model_width).astype(jnp.float32)
    normed, norm_back = jax.vjp(rms_norm, rows_float, gain_full)
    normed_low = normed.astype(jnp.bfloat16)
    mixed = mode_dot(normed_low, front_full, masks).astype(jnp.bfloat16)
    u_pre = mixed[:, :inner].reshape(seq_count, seg_len, inner)
    z_gate = mixed[:, inner:].astype(jnp.float32).reshape(seq_count, seg_len, inner)
    rim = passed_along(u_pre[:, seg_len - (taps - 1) :, :], "fsdp", 1)
    extended = jnp.concatenate([rim, u_pre], axis=1).astype(jnp.float32)
    u_act, conv_pull = jax.vjp(convolve, extended, conv_full, conv_shift)
    u_low = u_act.reshape(token_count, inner).astype(jnp.bfloat16)
    proj = mode_dot(u_low, select_full, masks)
    dt_rank = proj[:, :rank].astype(jnp.bfloat16)
    b_in = proj[:, rank : rank + states].reshape(seq_count, seg_len, states)
    c_out = proj[:, rank + states :].reshape(seq_count, seg_len, states)
    bias_rows = masks[:, 0:1] * bias_step[0]
    for copy_index in range(1, copies):
        bias_rows = bias_rows + masks[:, copy_index : copy_index + 1] * bias_step[copy_index]
    raw = (mode_dot(dt_rank, step_full, masks) + bias_rows).reshape(seq_count, seg_len, inner)
    delta = jax.nn.softplus(raw)
    rate = -jnp.exp(rate_log)
    end_local = final_state(delta, u_act, b_in, rate)
    decay = jnp.exp(rate[None, :, :] * jnp.sum(delta, axis=1)[:, None, :])
    identity = (jnp.ones_like(decay), jnp.zeros_like(end_local))
    carried = carried_in((decay, end_local), "fsdp", combine, identity, False)
    (gated, end_state), mixer_pull = jax.vjp(
        mixer_part, u_act, raw, b_in, c_out, z_gate, rate_log, skip_full, carried[1]
    )
    gated_low = gated.reshape(token_count, inner).astype(jnp.bfloat16)
    dout_low = out_grad.reshape(token_count, model_width)
    out_rows_sum = mode_dot(
        gated_low, lax.all_gather(out_weight, ("dp", "fsdp"), axis=1, tiled=True), masks
    )
    output = (
        (rows_float + out_rows_sum).astype(jnp.bfloat16).reshape(seq_count, seg_len, model_width)
    )
    outer_grad = mode_outer(gated_low, dout_low, masks)
    out_weight_grad = lax.psum_scatter(outer_grad, ("dp", "fsdp"), scatter_dimension=1, tiled=True)
    d_gated = mode_dot_back(
        dout_low, lax.all_gather(out_weight, ("dp", "fsdp"), axis=1, tiled=True), masks
    )
    front_full, select_full, step_full = (
        lax.all_gather(in_weight, ("dp", "fsdp"), axis=2, tiled=True),
        lax.all_gather(x_weight, ("dp", "fsdp"), axis=1, tiled=True),
        lax.all_gather(dt_weight, ("dp", "fsdp"), axis=2, tiled=True),
    )
    d_gated = d_gated.reshape(seq_count, seg_len, inner)
    d_y = d_gated * jax.nn.silu(z_gate)
    local_adjoint = adjoint_state(delta, c_out, d_y, rate)
    ahead = carried_in((decay, local_adjoint), "fsdp", combine, identity, True)
    d_u_mix, d_raw, d_b, d_c, d_z, rate_grad, skip_grad, unused_start = mixer_pull(
        (d_gated, ahead[1])
    )
    d_raw_low = d_raw.reshape(token_count, inner).astype(jnp.bfloat16)
    step_grad = mode_outer(dt_rank, d_raw_low, masks)
    sbias_grad = lax.dot_general(
        masks_low, d_raw_low, (((0,), (0,)), ((), ())), preferred_element_type=jnp.float32
    )
    d_rank = mode_dot_back(d_raw_low, step_full, masks)
    d_proj = jnp.concatenate(
        [d_rank, d_b.reshape(token_count, states), d_c.reshape(token_count, states)], axis=1
    ).astype(jnp.bfloat16)
    select_grad = mode_outer(u_low, d_proj, masks)
    d_u = d_u_mix.reshape(token_count, inner) + mode_dot_back(d_proj, select_full, masks)
    d_ext, conv_grad, cshift_grad = conv_pull(d_u.reshape(seq_count, seg_len, inner))
    rim_back = passed_along(d_ext[:, : taps - 1, :].astype(jnp.bfloat16), "fsdp", -1).astype(
        jnp.float32
    )
    d_u_pre = d_ext[:, taps - 1 :, :].at[:, seg_len - (taps - 1) :, :].add(rim_back)
    d_mixed = jnp.concatenate(
        [d_u_pre.reshape(token_count, inner), d_z.reshape(token_count, inner)], axis=1
    ).astype(jnp.bfloat16)
    front_grad = mode_outer(normed_low, d_mixed, masks)
    d_normed = mode_dot_back(d_mixed, front_full, masks)
    d_rows, gain_grad = norm_back(d_normed)
    input_grad = (dout_low.astype(jnp.float32) + d_rows).reshape(seq_count, seg_len, model_width)
    (
        in_weight_grad,
        x_weight_grad,
        dt_weight_grad,
        gain_grad_all,
        conv_weight_grad,
        conv_bias_grad,
        dt_bias_grad,
        log_rate_grad,
        skip_gain_grad,
    ) = (
        lax.psum_scatter(front_grad, ("dp", "fsdp"), scatter_dimension=2, tiled=True),
        lax.psum_scatter(select_grad, ("dp", "fsdp"), scatter_dimension=1, tiled=True),
        lax.psum_scatter(step_grad, ("dp", "fsdp"), scatter_dimension=2, tiled=True),
        lax.psum_scatter(gain_grad, ("dp", "fsdp"), scatter_dimension=0, tiled=True),
        lax.psum_scatter(conv_grad, ("dp", "fsdp"), scatter_dimension=1, tiled=True),
        lax.psum_scatter(cshift_grad, ("dp", "fsdp"), scatter_dimension=0, tiled=True),
        lax.psum_scatter(sbias_grad, ("dp", "fsdp"), scatter_dimension=1, tiled=True),
        lax.psum_scatter(rate_grad, ("dp", "fsdp"), scatter_dimension=1, tiled=True),
        lax.psum_scatter(skip_grad, ("dp", "fsdp"), scatter_dimension=0, tiled=True),
    )
    return (
        output,
        input_grad,
        gain_grad_all,
        in_weight_grad,
        conv_weight_grad,
        conv_bias_grad,
        x_weight_grad,
        dt_weight_grad,
        dt_bias_grad,
        log_rate_grad,
        skip_gain_grad,
        out_weight_grad,
    )


def solution(mesh):
    return jax.shard_map(
        shards,
        mesh=mesh,
        in_specs=(
            P("dp", "fsdp", None),
            P("dp", "fsdp"),
            P(("dp", "fsdp")),
            P(None, None, ("dp", "fsdp")),
            P(None, ("dp", "fsdp")),
            P(("dp", "fsdp")),
            P(None, ("dp", "fsdp"), None),
            P(None, None, ("dp", "fsdp")),
            P(None, ("dp", "fsdp")),
            P(None, ("dp", "fsdp")),
            P(("dp", "fsdp")),
            P(None, ("dp", "fsdp"), None),
            P("dp", "fsdp", None),
        ),
        out_specs=(
            P("dp", "fsdp", None),
            P("dp", "fsdp", None),
            P(("dp", "fsdp")),
            P(None, None, ("dp", "fsdp")),
            P(None, ("dp", "fsdp")),
            P(("dp", "fsdp")),
            P(None, ("dp", "fsdp"), None),
            P(None, None, ("dp", "fsdp")),
            P(None, ("dp", "fsdp")),
            P(None, ("dp", "fsdp")),
            P(("dp", "fsdp")),
            P(None, ("dp", "fsdp"), None),
        ),
        check_vma=False,
    )
```

profile of v0, /device:TPU:10, one launch (start us, length us, event | category | flops | bytes accessed | tf_op | source)
XLA Modules:
  0.0 5872.7 jit_solution(3607010022863627987)
XLA Ops:
  11.2 44.1 all-reduce.72
  55.6 53.3 all_gather.56
  109.0 66.4 %all-gather.3 = bf16[32,1,128]{2,1,0:T(2,128)(2,1)S(1)} all-gather(bf16[1,1,128]{2,1,0:T(2,128)(2,1)S(1)} %bitcast.2541), channel_id=1, replica_groups=mesh['dp'=8,'fsdp'=4] {'dp','fsdp'}, dimensions={0}, use_global_device_ids=true | all-gather | bytes 8448 | tf_op jit(solution)/shard_map/all_gather | solution.py:196
  175.4 71.1 %all_gather.54 = bf16[16,4096]{1,0:T(8,128)(2,1)S(1)} all-gather(bf16[16,128]{1,0:T(8,128)(2,1)S(1)} %copy-done.50), channel_id=1, replica_groups=mesh['dp'=8,'fsdp'=4] {'dp','fsdp'}, dimensions={1}, use_global_device_ids=true | all-gather | bytes 135168 | tf_op jit(solution)/shard_map/all_gather | solution.py:198
  246.6 60.8 %all_gather.61 = bf16[3,4096]{1,0:T(4,128)(2,1)S(1)} all-gather(bf16[3,128]{1,0:T(4,128)(2,1)S(1)} %copy-done.55), channel_id=1, replica_groups=mesh['dp'=8,'fsdp'=4] {'dp','fsdp'}, dimensions={1}, use_global_device_ids=true | all-gather | bytes 25344 | tf_op jit(solution)/shard_map/all_gather | solution.py:197
  307.4 63.8 %all-gather.4 = bf16[32,1,128]{2,1,0:T(2,128)(2,1)S(1)} all-gather(bf16[1,1,128]{2,1,0:T(2,128)(2,1)S(1)} %bitcast.2542), channel_id=1, replica_groups=mesh['dp'=8,'fsdp'=4] {'dp','fsdp'}, dimensions={0}, use_global_device_ids=true | all-gather | bytes 8448 | tf_op jit(solution)/shard_map/all_gather | solution.py:199
  371.8 10.2 fusion.243
  382.0 442.2 %all-gather.13.cloned.1.call-done = bf16[3,2048,8192]{2,1,0:T(8,128)(2,1)} async-done(((bf16[3,2048,256]{2,1,0:T(8,128)(2,1)}), bf16[3,2048,8192]{2,1,0:T(8,128)(2,1)}) %all-gather.13.cloned.1.call-update) | async-done | bytes 100663312 | tf_op jit(solution)/shard_map/all_gather | solution.py:191
  824.2 18.2 fusion.226
  842.4 21.4 fusion.225
  863.8 17.7 fusion.227
  884.6 11.4 fusion.242
  899.0 28.2 fusion.258
  935.5 15.7 all-gather.17.cloned.1.call-done
  971.1 9.4 copy.64
  980.8 51.9 while.98
  1042.5 48.0 while.100
  1099.2 116.2 %while.97 = (s32[]{:T(128)}, f32[1,16,4096]{2,1,0:T(8,128)S(1)}, f32[18,16,1,4096]{3,1,2,0:T(8,128)}, f32[18,1,16,4096]{3,2,1,0:T(8,128)}, f32[18,16,1,4096]{3,2...) while((s32[]{:T(128)}, f32[1,16,4096]{2,1,0:T(8,128)S(1)}, ...), condition=%wide.region_23.24_spmd, body=%wide.region_6.23_spmd.sunk | while | flops 9437201 | bytes 8265001 | solution.py:78
  1225.9 277.9 %while.102 = (s32[]{:T(128)}, f32[16,4096]{1,0:T(8,128)S(1)}, f32[1,16,4096]{2,1,0:T(8,128)S(1)}, f32[18,16,1,4096]{3,1,2,0:T(8,128)}, f32[18,16,1,4096]{3,1,2,0...) while((s32[]{:T(128)}, f32[16,4096]{1,0:T(8,128)S(1)}, ...), condition=%wide.region_93.94_spmd.clone, body=%wide.region_28.93_spmd.clone.sunk | while | flops 35462148 | bytes 25042140 | solution.py:78
  1526.7 21.1 multiply_reduce_fusion.66
  1571.9 38.2 fusion.228
  1626.5 16.8 fusion.278
  1643.4 16.6 fusion.279
  1660.0 17.7 fusion.287
  1683.6 70.5 %fusion.259 = f32[3,2048,8192]{2,1,0:T(8,128)} fusion(bf16[288,3]{0,1:T(4,128)(2,1)S(1)} %copy-done.16, bf16[288,2048]{1,0:T(8,128)(2,1)S(1)} %get-tuple-element.1631, bf16[288,4096]{1,0:T(8,128)(2,1)S(1)} %copy-done.7, bf16[288,4096]{1,0:T(8,128)(2,1)} %scatter-add.4), kind=kOutput, calls=%fused_computation.755 | convolution fusion | flops 29002235904 | bytes 207226560 | tf_op jit(solution)/shard_map/dot_general | solution.py:153
  1773.2 9.8 fusion.286
  1783.1 41.0 all-reduce.76
  1828.8 72.9 %reduce-scatter.18.cloned.1.call-done = f32[16,128]{1,0:T(8,128)} async-done(((f32[16,4096]{1,0:T(8,128)}), f32[16,128]{1,0:T(8,128)}) %reduce-scatter.18.cloned.1.call-update) | async-done | bytes 8208 | tf_op jit(solution)/shard_map/reduce_scatter | solution.py:304
  1901.8 134.2 %reduce-scatter.16.cloned.1.call-done = f32[3,128,128]{2,1,0:T(8,128)} async-done(((f32[3,128,4096]{2,1,0:T(8,128)}), f32[3,128,128]{2,1,0:T(8,128)}) %reduce-scatter.16.cloned.1.call-update) | async-done | bytes 196624 | tf_op jit(solution)/shard_map/reduce_scatter | solution.py:299
  2035.9 127.8 %reduce-scatter.14.cloned.1.call-done = f32[3,128,160]{1,2,0:T(8,128)} async-done(((f32[3,4096,160]{1,2,0:T(8,128)}), f32[3,128,160]{1,2,0:T(8,128)}) %reduce-scatter.14.cloned.1.call-update) | async-done | bytes 245776 | tf_op jit(solution)/shard_map/reduce_scatter | solution.py:298
  2163.7 2102.7 %reduce-scatter.20.cloned.1.call-done = f32[3,128,2048]{2,1,0:T(8,128)} async-done(((f32[3,4096,2048]{2,1,0:T(8,128)}), f32[3,128,2048]{2,1,0:T(8,128)}) %reduce-scatter.20.cloned.1.call-update) | async-done | bytes 3145744 | tf_op jit(solution)/shard_map/reduce_scatter | solution.py:247
  4266.4 1599.5 %reduce-scatter.12.cloned.1.call-done = f32[3,2048,256]{2,1,0:T(8,128)} async-done(((f32[3,2048,8192]{2,1,0:T(8,128)}), f32[3,2048,256]{2,1,0:T(8,128)}) %reduce-scatter.12.cloned.1.call-update) | async-done | bytes 6291472 | tf_op jit(solution)/shard_map/reduce_scatter | solution.py:297
  (2002 shorter events, 653.2 us)
Async XLA Ops:
  7.2 101.8 %copy-start.56 = (bf16[128]{0:T(256)(128)(2,1)S(1)}, bf16[128]{0:T(256)(128)(2,1)}, u32[]{:S(2)}) copy-start(bf16[128]{0:T(256)(128)(2,1)} %param.32) | copy-start | bytes 772
  7.2 168.2 %copy-start.50 = (bf16[16,128]{1,0:T(8,128)(2,1)S(1)}, bf16[16,128]{1,0:T(8,128)(2,1)}, u32[]{:S(2)}) copy-start(bf16[16,128]{1,0:T(8,128)(2,1)} %param.36) | copy-start | bytes 12292
  7.2 239.3 %copy-start.55 = (bf16[3,128]{1,0:T(4,128)(2,1)S(1)}, bf16[3,128]{1,0:T(4,128)(2,1)}, u32[]{:S(2)}) copy-start(bf16[3,128]{1,0:T(4,128)(2,1)} %param.35) | copy-start | bytes 2308
  7.3 300.2 %copy-start.57 = (bf16[128]{0:T(256)(128)(2,1)S(1)}, bf16[128]{0:T(256)(128)(2,1)}, u32[]{:S(2)}) copy-start(bf16[128]{0:T(256)(128)(2,1)} %param.37) | copy-start | bytes 772
  7.3 364.6 %copy-start.13 = (bf16[1,288,2048]{2,1,0:T(8,128)(2,1)S(1)}, bf16[1,288,2048]{2,1,0:T(8,128)(2,1)}, u32[]{:S(2)}) copy-start(bf16[1,288,2048]{2,1,0:T(8,128)(2,1)} %param.39) | copy-start | bytes 3538948
  7.3 364.5 %all-gather.19.cloned.1.call-start = ((), (), s32[]{:S(2)}) async-start(), calls=%async_computation.10 | async-start | bytes 51904512 | tf_op jit(solution)/shard_map/all_gather | solution.py:241
  8.0 816.2 %all-gather.13.cloned.1.call-start = ((), (), s32[]{:S(2)}) async-start(), calls=%async_computation.7 | async-start | bytes 103809024 | tf_op jit(solution)/shard_map/all_gather | solution.py:191
  8.8 921.1 %all-gather.15.cloned.1.call-start = ((), (), s32[]{:S(2)}) async-start(), calls=%async_computation.8 | async-start | bytes 4055040 | tf_op jit(solution)/shard_map/all_gather | solution.py:192
  9.5 941.8 %all-gather.17.cloned.1.call-start = ((), (), s32[]{:S(2)}) async-start(), calls=%async_computation.9 | async-start | bytes 3244032 | tf_op jit(solution)/shard_map/all_gather | solution.py:193
  10.1 1081.2 %all-gather.21.cloned.1.call-start = ((), (), s32[]{:S(2)}) async-start(), calls=%async_computation.16 | async-start | bytes 1310720 | tf_op jit(solution)/shard_map/all_gather | solution.py:19
  10.9 1511.5 %copy-start.25 = (f32[288]{0:T(512)}, f32[288]{0:T(512)S(1)}, u32[]{:S(2)}) copy-start(f32[288]{0:T(512)S(1)} %get-tuple-element.1169) | copy-start | bytes 3460
  10.9 1615.7 %copy-start.51 = (f32[288]{0:T(512)}, f32[288]{0:T(512)S(1)}, u32[]{:S(2)}) copy-start(f32[288]{0:T(512)S(1)} %get-tuple-element.1167) | copy-start | bytes 3460
  10.9 1632.4 %copy-start.27 = (f32[288]{0:T(512)}, f32[288]{0:T(512)S(1)}, u32[]{:S(2)}) copy-start(f32[288]{0:T(512)S(1)} %get-tuple-element.1168) | copy-start | bytes 3460
  55.2 808.5 %copy-start.30 = (f32[2048]{0:T(1024)}, f32[2048]{0:T(1024)S(1)}, u32[]{:S(2)}) copy-start(f32[2048]{0:T(1024)S(1)} %convert_element_type.135) | copy-start | bytes 24580
  55.6 326.4 %copy-start.33 = (f32[288]{0:T(512)}, f32[288]{0:T(512)S(1)}, u32[]{:S(2)}) copy-start(f32[288]{0:T(512)S(1)} %fusion.289) | copy-start | bytes 3460
  55.6 808.2 %copy-start.47 = (f32[288]{0:T(512)}, f32[288]{0:T(512)S(1)}, u32[]{:S(2)}) copy-start(f32[288]{0:T(512)S(1)} %fusion.320) | copy-start | bytes 3460
  109.0 790.0 %copy-start.39 = (f32[1,4096]{1,0:T(1,128)}, f32[1,4096]{1,0:T(1,128)S(1)}, u32[]{:S(2)}) copy-start(f32[1,4096]{1,0:T(1,128)S(1)} %get-tuple-element.1641) | copy-start | bytes 49156
  109.0 790.0 %copy-start.41 = (f32[1,4096]{1,0:T(1,128)}, f32[1,4096]{1,0:T(1,128)S(1)}, u32[]{:S(2)}) copy-start(f32[1,4096]{1,0:T(1,128)S(1)} %get-tuple-element.1642) | copy-start | bytes 49156
  109.0 790.0 %copy-start.43 = (f32[1,4096]{1,0:T(1,128)}, f32[1,4096]{1,0:T(1,128)S(1)}, u32[]{:S(2)}) copy-start(f32[1,4096]{1,0:T(1,128)S(1)} %get-tuple-element.1643) | copy-start | bytes 49156
  109.0 790.0 %copy-start.45 = (f32[1,4096]{1,0:T(1,128)}, f32[1,4096]{1,0:T(1,128)S(1)}, u32[]{:S(2)}) copy-start(f32[1,4096]{1,0:T(1,128)S(1)} %get-tuple-element.1644) | copy-start | bytes 49156
  881.7 14.3 collective-permute-start
  961.5 129.8 %all-gather.23.cloned.1.call-start = ((), (), s32[]{:S(2)}) async-start(), calls=%async_computation.17 | async-start | bytes 1310720 | tf_op jit(solution)/shard_map/all_gather | solution.py:19
  1042.4 172.9 %all-gather.25.cloned.1.call-start = ((), (), s32[]{:S(2)}) async-start(), calls=%async_computation.18 | async-start | bytes 1310720 | tf_op jit(solution)/shard_map/all_gather | solution.py:19
  1091.2 734.6 %reduce-scatter.24.cloned.1.call-start = ((), (), s32[]{:S(2)}) async-start(), calls=%async_computation.20 | async-start | bytes 2162688
  1099.2 116.2 %copy-start.1 = (f32[1,16,4096]{2,1,0:T(8,128)S(1)}, f32[1,16,4096]{2,1,0:T(8,128)}, u32[]{:S(2)}) copy-start(f32[1,16,4096]{2,1,0:T(8,128)} %custom-call.3) | copy-start | bytes 786436
  1512.8 314.5 %reduce-scatter.22.cloned.1.call-start = ((), (), s32[]{:S(2)}) async-start(), calls=%async_computation.19 | async-start | bytes 2162688
  1549.9 351.9 %reduce-scatter.18.cloned.1.call-start = ((), (), s32[]{:S(2)}) async-start(), calls=%async_computation.14 | async-start | bytes 270336 | tf_op jit(solution)/shard_map/reduce_scatter | solution.py:304
  1550.7 485.2 %reduce-scatter.16.cloned.1.call-start = ((), (), s32[]{:S(2)}) async-start(), calls=%async_computation.13 | async-start | bytes 6488064 | tf_op jit(solution)/shard_map/reduce_scatter | solution.py:299
  1555.9 607.8 %reduce-scatter.14.cloned.1.call-start = ((), (), s32[]{:S(2)}) async-start(), calls=%async_computation.12 | async-start | bytes 8110080 | tf_op jit(solution)/shard_map/reduce_scatter | solution.py:298
  1563.4 2703.0 %reduce-scatter.20.cloned.1.call-start = ((), (), s32[]{:S(2)}) async-start(), calls=%async_computation.15 | async-start | bytes 103809024 | tf_op jit(solution)/shard_map/reduce_scatter | solution.py:247
  1610.2 4255.8 %reduce-scatter.12.cloned.1.call-start = ((), (), s32[]{:S(2)}) async-start(), calls=%async_computation.11 | async-start | bytes 207618048 | tf_op jit(solution)/shard_map/reduce_scatter | solution.py:297
  1617.8 7.1 collective-permute-start.1
  (43 other events, 519.7 us)
Sparse Core Ops, SparseCore 0:
  11.1 277.6 all-gather.18
  290.3 533.9 all-gather.12
  827.1 63.4 all-gather.14
  893.2 58.0 all-gather.16
  961.6 27.0 all-gather.20
  1042.5 27.0 all-gather.22
  1091.3 26.9 all-gather.24
  1512.9 121.4 reduce-scatter.23
  1636.8 132.9 reduce-scatter.21
  1772.5 129.2 reduce-scatter.17
  1908.9 126.9 reduce-scatter.15
  2042.0 121.6 reduce-scatter.13
  2166.7 2099.6 reduce-scatter.19
  4274.4 1591.4 reduce-scatter.11
where the time goes:
time: 5890 us; the launch traced here: 5870 us
  waiting for transfers between devices  4500 us (76%)
  blocking collectives  401 us (7%)
  matrix products  349 us (6%)
  other arithmetic  323 us (5%)
  local copies, waits for them, and re-layouts  266 us (5%)
    reduce_scatter x1, waiting for transfers between devices, shards(): lax.psum_scatter(outer_grad, ('dp', 'fsdp'), scatter_dimension=1, tiled=T...  2100 us
    reduce_scatter x1, waiting for transfers between devices, shards(): lax.psum_scatter(front_grad, ('dp', 'fsdp'), scatter_dimension=2, tiled=T...  1600 us
    all_gather x1, waiting for transfers between devices, shards(): lax.all_gather(in_weight, ('dp', 'fsdp'), axis=2, tiled=True)  442 us
    reduce_scatter x1, waiting for transfers between devices, shards(): lax.psum_scatter(step_grad, ('dp', 'fsdp'), scatter_dimension=2, tiled=True)  134 us
    reduce_scatter x1, waiting for transfers between devices, shards(): lax.psum_scatter(select_grad, ('dp', 'fsdp'), scatter_dimension=1, tiled=...  128 us
    dot_general x4, matrix products, mode_outer(): lax.dot_general(spread, right, (((0,), (0,)), ((), ())), preferred_elemen...  119 us
  transfers between devices with their start and end apart: 16, of which 8 were waited for; matrix products, arithmetic and copies ran while one was open for 11% of the time, Pallas kernels for 0%

commit v1 on v0

v1 whole, which is shorter than its diff:
```python
import functools
import math

import jax
import jax.numpy as jnp
from jax import lax
from jax.experimental import pallas as pl
from jax.experimental.pallas import tpu as pltpu
from jax.sharding import PartitionSpec as P

epsilon = 1e-05
LANES = 128
SUB = 8


def spread_maps(parts_ref, ones_ref, spread, first, last):
    chunk = spread.shape[0]
    for n in range(first, last, 2):
        both = jnp.dot(
            parts_ref[...],
            ones_ref[:, n * LANES : (n + 2) * LANES],
            preferred_element_type=jnp.float32,
        )
        spread[:, n] = both[:, :LANES].reshape(chunk, SUB, LANES)
        spread[:, n + 1] = both[:, LANES:].reshape(chunk, SUB, LANES)


def lane_blocks(width):
    return [pl.ds(start, LANES) for start in range(0, width, LANES)]


def state_blocks(states):
    return [(0, states // 2), (states // 2, states)]


def end_kernel(d_ref, u_ref, parts_ref, ones_ref, rate_ref, end_ref, sum_ref, spread):
    @pl.when(pl.program_id(1) == 0)
    def _():
        end_ref[...] = jnp.zeros_like(end_ref)
        sum_ref[...] = jnp.zeros_like(sum_ref)

    chunk, states = d_ref.shape[0], rate_ref.shape[0]
    spread_maps(parts_ref, ones_ref, spread, 0, states)
    for lanes in lane_blocks(d_ref.shape[2]):
        sum_ref[:, lanes] += jnp.sum(d_ref[:, :, lanes], axis=0)
        rate = rate_ref[:, :, lanes]

        def body(t, state):
            d, u = d_ref[t, :, lanes], u_ref[t, :, lanes]
            return jnp.exp2(d[None] * rate) * state + (d * u)[None] * spread[t, :states]

        end_ref[:, :, lanes] = lax.fori_loop(0, chunk, body, end_ref[:, :, lanes], unroll=4)


def ahead_kernel(d_ref, y_ref, parts_ref, ones_ref, rate_ref, out_ref, spread):
    @pl.when(pl.program_id(1) == 0)
    def _():
        out_ref[...] = jnp.zeros_like(out_ref)

    chunk, states = d_ref.shape[0], rate_ref.shape[0]
    spread_maps(parts_ref, ones_ref, spread, states, 2 * states)
    for lanes in lane_blocks(d_ref.shape[2]):
        rate = rate_ref[:, :, lanes]

        def body(k, grad):
            t = chunk - 1 - k
            d, dy = d_ref[t, :, lanes], y_ref[t, :, lanes]
            return jnp.exp2(d[None] * rate) * (grad + dy[None] * spread[t, states:])

        out_ref[:, :, lanes] = lax.fori_loop(0, chunk, body, out_ref[:, :, lanes], unroll=4)


def forward_kernel(
    d_ref, u_ref, parts_ref, ones_ref, rate_ref, start_ref, *refs
):
    y_ref, kept_ref, state_ref, spread = refs[-4:]

    @pl.when(pl.program_id(1) == 0)
    def _():
        state_ref[...] = start_ref[...]

    chunk, states = d_ref.shape[0], rate_ref.shape[0]
    spread_maps(parts_ref, ones_ref, spread, 0, 2 * states)
    kept_ref[0] = state_ref[...]
    for lanes in lane_blocks(d_ref.shape[2]):
        rate = rate_ref[:, :, lanes]

        def body(t, state):
            d, u = d_ref[t, :, lanes], u_ref[t, :, lanes]
            state = jnp.exp2(d[None] * rate) * state + (d * u)[None] * spread[t, :states]
            y_ref[t, :, lanes] = jnp.sum(state * spread[t, states:], axis=0)
            return state

        state_ref[:, :, lanes] = lax.fori_loop(0, chunk, body, state_ref[:, :, lanes], unroll=4)


def backward_kernel(
    d_ref,
    u_ref,
    y_ref,
    parts_ref,
    ones_ref,
    rate_ref,
    kept_ref,
    start_ref,
    *refs,
):
    du_ref, dd_ref, dmaps_ref, drate_ref, grad_ref, spread, held, factors, partial = refs[-9:]

    @pl.when(pl.program_id(1) == 0)
    def _():
        grad_ref[...] = start_ref[...]
        drate_ref[...] = jnp.zeros_like(drate_ref)

    chunk, states = d_ref.shape[0], rate_ref.shape[0]
    natural = math.log(2.0)
    spread_maps(parts_ref, ones_ref, spread, 0, 2 * states)
    for index, lanes in enumerate(lane_blocks(d_ref.shape[2])):
        for low, high in state_blocks(states):
            rate = rate_ref[low:high, :, lanes]
            held[0] = kept_ref[0, low:high, :, lanes]

            def forward(t, state):
                d, u = d_ref[t, :, lanes], u_ref[t, :, lanes]
                factor = jnp.exp2(d[None] * rate)
                state = factor * state + (d * u)[None] * spread[t, low:high]
                factors[t] = factor
                held[t + 1] = state
                return state

            lax.fori_loop(0, chunk, forward, held[0], unroll=4)

            def backward(k, carry):
                t = chunk - 1 - k
                ahead, drate = carry
                d, u, dy = d_ref[t, :, lanes], u_ref[t, :, lanes], y_ref[t, :, lanes]
                grad = spread[t, states + low : states + high] * dy[None] + ahead
                part_b = (d * u)[None] * grad
                part_c = dy[None] * held[t + 1]
                if index == 0:
                    partial[t, low:high] = part_b
                    partial[t, states + low : states + high] = part_c
                else:
                    partial[t, low:high] += part_b
                    partial[t, states + low : states + high] += part_c
                through = jnp.sum(grad * spread[t, low:high], axis=0)
                ahead = factors[t] * grad
                moved = ahead * held[t]
                du, dd = d * through, natural * jnp.sum(moved * rate, axis=0) + u * through
                if low == 0:
                    du_ref[t, :, lanes] = du
                    dd_ref[t, :, lanes] = dd
                else:
                    du_ref[t, :, lanes] += du
                    dd_ref[t, :, lanes] += dd
                return ahead, drate + d[None] * moved

            ahead, drate = lax.fori_loop(
                0,
                chunk,
                backward,
                (grad_ref[low:high, :, lanes], drate_ref[low:high, :, lanes]),
                unroll=4,
            )
            grad_ref[low:high, :, lanes] = ahead
            drate_ref[low:high, :, lanes] = drate

    column = lax.broadcasted_iota(jnp.int32, (SUB, LANES), 1)

    def gather(t, _):
        total = jnp.zeros((SUB, LANES), jnp.float32)
        for n in range(2 * states):
            total = jnp.where(column == n, jnp.sum(partial[t, n], axis=1, keepdims=True), total)
        dmaps_ref[t] = total[:, : 2 * states]
        return 0

    lax.fori_loop(0, chunk, gather, 0, unroll=4)


def scan_call(kernel, delta, states, reverse, ins, outs, scratch, cost, after=()):
    length, count, width = delta.shape
    chunk = math.gcd(16, length)
    steps = length // chunk

    def at(t):
        return steps - 1 - t if reverse else t

    specs = {
        "rows": (
            pl.BlockSpec((chunk, SUB, width), lambda b, t: (at(t), b, 0)),
            (length, count, width),
        ),
        "maps": (
            pl.BlockSpec((chunk, SUB, 2 * states), lambda b, t: (at(t), b, 0)),
            (length, count, 2 * states),
        ),
        "parts": (
            pl.BlockSpec((None, chunk * SUB, 6 * states), lambda b, t: (b, at(t), 0)),
            (count // SUB, length * SUB, 6 * states),
        ),
        "ones": (
            pl.BlockSpec((6 * states, 2 * states * LANES), lambda b, t: (0, 0)),
            (6 * states, 2 * states * LANES),
        ),
        "state": (
            pl.BlockSpec((states, SUB, width), lambda b, t: (0, b, 0)),
            (states, count, width),
        ),
        "rate": (
            pl.BlockSpec((states, SUB, width), lambda b, t: (0, 0, 0)),
            (states, SUB, width),
        ),
        "kept": (
            pl.BlockSpec((1, states, SUB, width), lambda b, t: (at(t), 0, b, 0)),
            (steps, states, count, width),
        ),
        "sum": (pl.BlockSpec((SUB, width), lambda b, t: (b, 0)), (count, width)),
    }
    sizes = {
        "spread": pltpu.VMEM((chunk, 2 * states, SUB, LANES), jnp.float32),
        "held": pltpu.VMEM((chunk + 1, states // 2, SUB, LANES), jnp.float32),
        "factors": pltpu.VMEM((chunk, states // 2, SUB, LANES), jnp.float32),
        "state": pltpu.VMEM((states, SUB, width), jnp.float32),
    }
    return pl.pallas_call(
        kernel,
        grid=(count // SUB, steps),
        in_specs=[specs[name][0] for name, _ in ins]
        + [pl.BlockSpec(memory_space=pl.ANY) for _ in after],
        out_specs=[specs[name][0] for name in outs],
        out_shape=[jax.ShapeDtypeStruct(specs[name][1], jnp.float32) for name in outs],
        scratch_shapes=[sizes[name] for name in scratch],
        compiler_params=pltpu.CompilerParams(vmem_limit_bytes=40 * 1024 * 1024),
        cost_estimate=pl.CostEstimate(
            flops=length * count * width * states * cost * 300,
            bytes_accessed=length * count * width * 4 * (len(ins) + len(outs)),
            transcendentals=length * count * width * states,
        ),
    )(*[value for _, value in ins], *after)


def masked(left, masks):
    return left[:, None, :] * masks.astype(left.dtype)[:, :, None]


def mode_dot(left, weight, masks):
    return lax.dot_general(
        masked(left, masks), weight, (((1, 2), (0, 1)), ((), ())), preferred_element_type=jnp.float32
    )


def mode_dot_back(left, weight, masks):
    return lax.dot_general(
        masked(left, masks), weight, (((1, 2), (0, 2)), ((), ())), preferred_element_type=jnp.float32
    )


def mode_outer(left, right, masks):
    return lax.dot_general(
        masked(left, masks), right, (((0,), (0,)), ((), ())), preferred_element_type=jnp.float32
    )


def exchanged(value, axis, mask):
    count = lax.axis_size(axis)
    return lax.ppermute(value, axis, [(source, source ^ mask) for source in range(count)])


def gathered(value, axis, dimension):
    pieces = [value] + [exchanged(value, axis, m) for m in range(1, lax.axis_size(axis))]
    return jnp.concatenate(pieces, axis=dimension)


def piece_of(pieces, index):
    return lax.dynamic_index_in_dim(pieces, index, axis=0, keepdims=False)


def then(*values):
    return lax.optimization_barrier(values)


def core_sent(pieces, kind):
    core = lax.axis_index("dp") % 2
    pairs = pieces.reshape((pieces.shape[0] // 2, 2) + pieces.shape[1:])
    kept = lax.dynamic_index_in_dim(pairs, core, axis=1, keepdims=False)
    other = lax.dynamic_index_in_dim(pairs, 1 - core, axis=1, keepdims=False)
    return kept, exchanged(other.astype(kind), "dp", 1)


def chips_sent(kept, other, kind):
    place = lax.axis_index("dp") // 2
    both = kept.astype(jnp.float32) + other.astype(jnp.float32)
    sent = [piece_of(both, place ^ m).astype(kind) for m in range(1, both.shape[0])]
    return [piece_of(both, place)], sent


def chips_received(sent):
    return [exchanged(value, "dp", 2 * (m + 1)) for m, value in enumerate(sent)]


def summed(values):
    total = values[0].astype(jnp.float32)
    for value in values[1:]:
        total = total + value.astype(jnp.float32)
    return total


def chips_gathered(value):
    return [value] + [
        exchanged(value, "dp", 2 * m) for m in range(1, lax.axis_size("dp") // 2)
    ]


def core_gathered(column):
    here = lax.axis_index("dp")
    core, place = here % 2, here // 2
    column = jnp.stack(column)
    column = jnp.stack([piece_of(column, place ^ k) for k in range(column.shape[0])])
    other = exchanged(column, "dp", 1)
    both = [jnp.where(core == 0, column, other), jnp.where(core == 0, other, column)]
    return jnp.stack(both, axis=1).reshape((-1,) + column.shape[1:])


def in_order(value, blocks):
    here = lax.axis_index("fsdp")
    pieces = jnp.stack(jnp.split(value, blocks, axis=-1))
    return jnp.concatenate([piece_of(pieces, here ^ k) for k in range(blocks)], axis=-1)


def to_workers(block, first):
    half = lax.axis_size("dp") * lax.axis_size("fsdp") // 2
    size = block.shape[2] // 2
    low, high = block[:, :, :size], block[:, :, size:]
    even = lax.ppermute(low, ("dp", "fsdp"), [(first + s, 2 * s) for s in range(half)])
    odd = lax.ppermute(high, ("dp", "fsdp"), [(first + s, 2 * s + 1) for s in range(half)])
    return even + odd


def to_owners(piece, first):
    half = lax.axis_size("dp") * lax.axis_size("fsdp") // 2
    even = lax.ppermute(piece, ("dp", "fsdp"), [(2 * s, first + s) for s in range(half)])
    odd = lax.ppermute(piece, ("dp", "fsdp"), [(2 * s + 1, first + s) for s in range(half)])
    return even, odd


def shifted(value, axis, steps):
    count = lax.axis_size(axis)
    initial, last = (max(0, -steps), min(count, count - steps))
    return lax.ppermute(value, axis, [(source, source + steps) for source in range(initial, last)])


def carried_in(decays, ends, reverse):
    count, here = lax.axis_size("fsdp"), lax.axis_index("fsdp")
    decays, ends = jnp.stack(decays), jnp.stack(ends)
    total = jnp.zeros_like(ends[0])
    for k in range(count - 1):
        at = count - 1 - k if reverse else k
        reached = at > here if reverse else at < here
        new = piece_of(decays, here ^ at) * total + piece_of(ends, here ^ at)
        total = jnp.where(reached, new, total)
    return total


def convolve(extended, conv_full, conv_shift, length):
    total = conv_shift
    for tap in range(conv_full.shape[0]):
        total = total + conv_full[tap] * extended[tap : tap + length]
    return total


def swap(value):
    return jnp.swapaxes(value, 0, 1)


def shards(
    inputs,
    modality,
    gain,
    in_weight,
    conv_weight,
    conv_bias,
    x_weight,
    dt_weight,
    dt_bias,
    log_rate,
    skip_gain,
    out_weight,
    out_grad,
):
    seq_count, length, model = inputs.shape
    copies, rank, block = in_weight.shape[0], dt_weight.shape[1], dt_weight.shape[2]
    taps, states = conv_weight.shape[0], log_rate.shape[0]
    groups, parts = lax.axis_size("dp"), lax.axis_size("fsdp")
    count = groups * seq_count
    tokens = count * length
    width = parts * block
    low, full = jnp.bfloat16, jnp.float32

    gain_row = jnp.pad(gain, (0, block - gain.shape[0]))[None]
    packed = jnp.concatenate(
        [
            gain_row,
            conv_weight,
            conv_bias[None],
            dt_bias,
            log_rate,
            skip_gain[None],
            dt_weight.reshape(copies * rank, block),
            jnp.transpose(x_weight, (0, 2, 1)).reshape(-1, block),
        ],
        axis=0,
    )
    packed = in_order(lax.all_gather(packed, "fsdp", axis=1, tiled=True), parts)
    sizes = [1, taps, 1, copies, states, 1, copies * rank, copies * (rank + 2 * states)]
    rows, at = [], 0
    for size in sizes:
        rows.append(packed[at : at + size])
        at += size
    gain_part = in_order(rows[0].reshape(parts, block)[:, : gain.shape[0]].reshape(-1), parts)
    conv_full, conv_shift = rows[1].astype(full), rows[2][0].astype(full)
    bias_step, rate_log, skip_full = rows[3].astype(full), rows[4].astype(full), rows[5][0].astype(full)
    step_full = rows[6].reshape(copies, rank, width)
    select_full = rows[7].reshape(copies, rank + 2 * states, width)

    small = jnp.concatenate([gain_part, modality.reshape(-1).astype(low)])
    small = lax.all_gather(small[None], "dp", axis=0, tiled=True)
    gain_full = small[:, : gain_part.shape[0]].reshape(model).astype(full)
    kinds = small[:, gain_part.shape[0] :].reshape(count, length)
    copy_ids = jnp.arange(copies, dtype=low)

    def masks_of(values):
        return (values.reshape(tokens)[:, None] == copy_ids[None, :]).astype(full)

    masks, masks_t = masks_of(kinds), masks_of(swap(kinds))

    x_all = lax.all_gather(inputs, "dp", axis=0, tiled=True).reshape(tokens, model)
    front_block = to_workers(in_weight, 0)
    out_parts = [out_weight] + [exchanged(out_weight, "fsdp", m) for m in range(1, parts)]
    out_parts, gate_from = then(out_parts, in_weight)
    gate_block = to_workers(gate_from, groups * parts // 2)
    x_all, g_sent = then(x_all, out_grad)
    g_all = lax.all_gather(g_sent, "dp", axis=0, tiled=True).reshape(tokens, model)
    front_full = gathered(front_block, "fsdp", 2)
    out_full = jnp.concatenate(out_parts, axis=1)

    x_float = x_all.astype(full)
    inverse = lax.rsqrt(jnp.mean(x_float * x_float, axis=-1, keepdims=True) + epsilon)
    normed = (x_float * inverse * gain_full).astype(low)

    def by_time(value):
        return swap(value.reshape(count, length, value.shape[1]))

    def by_sequence(value):
        return swap(value).reshape(tokens, value.shape[2])

    u_pre = by_time(mode_dot(normed, front_full, masks).astype(low))
    rim = in_order(shifted(in_order(u_pre[length - (taps - 1) :], parts), "fsdp", 1), parts)
    rim, gate_block = then(rim, gate_block)
    gate_parts = [gate_block] + [exchanged(gate_block, "fsdp", m) for m in range(1, parts)]
    extended = jnp.concatenate([rim, u_pre], axis=0).astype(full)
    pre_conv = convolve(extended, conv_full, conv_shift, length)
    u_act = jax.nn.silu(pre_conv)
    u_low = u_act.astype(low).reshape(tokens, width)
    proj = mode_dot_back(u_low, select_full, masks_t)
    proj, g_then = then(proj, g_all)
    kept_part, other = core_sent(proj.reshape(groups, tokens // groups, -1), full)
    d_gated = mode_dot_back(g_then, out_full, masks)
    other, d_gated = then(other, d_gated)
    own, sent = chips_sent(kept_part, other, full)
    column = chips_gathered(summed(own + chips_received(sent)))
    column, gate_parts = then(column, gate_parts)
    proj = core_gathered(column).reshape(tokens, -1)
    dt_rank = proj[:, :rank].astype(low)
    maps = proj[:, rank:]
    top = lax.reduce_precision(maps, 8, 7)
    middle = lax.reduce_precision(maps - top, 8, 7)
    thirds = jnp.concatenate([top, middle, maps - top - middle], axis=1).astype(low)
    thirds = jnp.moveaxis(thirds.reshape(length, count // SUB, SUB, 6 * states), 1, 0)
    thirds = thirds.reshape(count // SUB, length * SUB, 6 * states)
    ones = (
        jnp.arange(6 * states)[:, None] % (2 * states) == jnp.arange(2 * states * LANES)[None] // LANES
    ).astype(low)
    bias_rows = masks_t[:, 0:1] * bias_step[0]
    for copy_index in range(1, copies):
        bias_rows = bias_rows + masks_t[:, copy_index : copy_index + 1] * bias_step[copy_index]
    raw = (mode_dot(dt_rank, step_full, masks_t) + bias_rows).reshape(length, count, width)
    delta = jax.nn.softplus(raw)
    rate = -jnp.exp(rate_log)
    scaled = jnp.broadcast_to((rate * math.log2(math.e))[:, None, :], (states, SUB, width))

    def exchange_edge(edge):
        edges = [edge]
        for m in range(1, parts):
            pieces = jnp.split(exchanged(edge, "fsdp", m), parts, axis=2)
            edges.append(jnp.concatenate([pieces[q ^ m] for q in range(parts)], axis=2))
        return edges

    common = [("parts", thirds), ("ones", ones), ("rate", scaled)]
    end, total = scan_call(
        end_kernel, delta, states, False,
        [("rows", delta), ("rows", u_act)] + common, ["state", "sum"], ["spread"], 4,
    )
    edge, normed_then, gate_parts = then(
        jnp.concatenate([end, total[None]], axis=0), normed, gate_parts
    )
    edges = exchange_edge(edge)
    gate_full = jnp.concatenate(gate_parts, axis=2)
    z_low = mode_dot(normed_then, gate_full, masks).astype(low)
    edges, z_low = then(edges, z_low)
    z_gate = by_time(z_low).astype(full)
    gate = jax.nn.silu(z_gate)
    d_gated = by_time(d_gated)
    d_y = d_gated * gate
    decays = [jnp.exp(rate[:, None, :] * other[states][None]) for other in edges]
    start = carried_in(decays, [other[:states] for other in edges], False)
    (ahead,) = scan_call(
        ahead_kernel, delta, states, True,
        [("rows", delta), ("rows", d_y)] + common, ["state"], ["spread"], 4,
    )
    aheads = exchange_edge(ahead)
    y_scan, kept = scan_call(
        forward_kernel, delta, states, False,
        [("rows", delta), ("rows", u_act)] + common + [("state", start)],
        ["rows", "kept"], ["state", "spread"], 6, after=(ahead,),
    )
    y_scan, aheads = then(y_scan, aheads)
    final = carried_in(decays, aheads, True)
    mixed_out = y_scan + skip_full * u_act
    gated = by_sequence((mixed_out * gate).astype(low))
    sig_z = jax.nn.sigmoid(z_gate)
    d_z = d_gated * mixed_out * (sig_z * (1.0 + z_gate * (1.0 - sig_z)))
    d_gate = by_sequence(d_z.astype(low))

    def lowered(grad):
        return [grad[:, 0]] + [grad[:, m].astype(low) for m in range(1, parts)]

    def fsdp_received(pieces):
        return pieces[:1] + [exchanged(pieces[m], "fsdp", m) for m in range(1, parts)]

    gate_grad = lowered(mode_outer(d_gate, normed, masks).reshape(copies, parts, block, model))
    gate_grad, gated = then(gate_grad, gated)
    out_sent = mode_dot(gated, out_full, masks).astype(low).reshape(count, length, model)
    out_sent, gated = then(out_sent, gated)
    out_rows = lax.psum_scatter(out_sent, "dp", scatter_dimension=0, tiled=True)

    outer_grad = lowered(mode_outer(gated, g_all, masks).reshape(copies, parts, block, model))
    d_u_scan, d_delta, d_maps, rate_part = scan_call(
        backward_kernel, delta, states, True,
        [("rows", delta), ("rows", u_act), ("rows", d_y)] + common
        + [("kept", kept), ("state", final)],
        ["rows", "rows", "maps", "state"], ["state", "spread", "held", "factors", "spread"], 16,
        after=(out_sent, gate_grad[-1], outer_grad[-1]),
    )
    gate_received, outer_received = fsdp_received(gate_grad), fsdp_received(outer_grad)
    d_u_scan, d_delta, d_maps, rate_part, gate_received, outer_received = then(
        d_u_scan, d_delta, d_maps, rate_part, gate_received, outer_received
    )
    gate_piece = jnp.swapaxes(summed(gate_received).astype(low), 1, 2)
    out_weight_grad = summed(outer_received)
    rate_grad = rate * jnp.sum(rate_part, axis=1)
    d_raw = (d_delta * jax.nn.sigmoid(raw)).astype(low).reshape(tokens, width)
    d_rank = mode_dot_back(d_raw, step_full, masks_t)
    d_proj = jnp.concatenate([d_rank, d_maps.reshape(tokens, 2 * states)], axis=1)
    d_proj, d_gate = then(d_proj, d_gate)
    kept_part, other = core_sent(d_proj.reshape(groups, tokens // groups, -1), full)
    d_normed_gate = mode_dot_back(d_gate, gate_full, masks)
    skip_grad = jnp.sum(d_y * u_act, axis=(0, 1))
    step_grad = mode_outer(dt_rank, d_raw, masks_t)
    sbias_grad = lax.dot_general(
        masks_t.astype(low), d_raw, (((0,), (0,)), ((), ())), preferred_element_type=full
    )
    other, d_normed_gate = then(other, d_normed_gate)
    own, sent = chips_sent(kept_part, other, full)
    own = summed(own + chips_received(sent)).astype(low)
    d_proj = core_gathered(chips_gathered(own)).reshape(tokens, -1)
    d_proj, gate_piece, skip_grad, step_grad, sbias_grad, out_rows = then(
        d_proj, gate_piece, skip_grad, step_grad, sbias_grad, out_rows
    )
    output = (inputs.astype(full) + out_rows.astype(full)).astype(low)
    gate_even, gate_odd = to_owners(gate_piece, groups * parts // 2)
    d_u = (
        d_u_scan
        + skip_full * d_y
        + mode_dot(d_proj, select_full, masks_t).reshape(length, count, width)
    )
    sig_c = jax.nn.sigmoid(pre_conv)
    d_conv = d_u * (sig_c * (1.0 + pre_conv * (1.0 - sig_c)))
    rim_back = shifted(in_order(d_conv[: taps - 1].astype(low), parts), "fsdp", -1)
    d_ahead = jnp.concatenate([d_conv, in_order(rim_back, parts).astype(full)], axis=0)
    d_u_pre = convolve(d_ahead, conv_full[::-1], 0.0, length)
    d_front = by_sequence(d_u_pre.astype(low))
    d_normed = d_normed_gate + mode_dot_back(d_front, front_full, masks)
    d_sent = d_normed.astype(low).reshape(groups, seq_count, length, model)
    d_sent, d_front, gate_even, gate_odd = then(d_sent, d_front, gate_even, gate_odd)
    kept_part, other = core_sent(d_sent, low)
    gain_part = jnp.sum(d_normed * x_float * inverse, axis=0)
    gain_part, d_front = then(gain_part, d_front)
    gain_kept, gain_other = core_sent(gain_part.reshape(groups, -1), full)
    gain_own, gain_sent = chips_sent(gain_kept, gain_other, full)
    gain_part = summed(gain_own + chips_received(gain_sent))
    front_pieces = lowered(mode_outer(d_front, normed, masks).reshape(copies, parts, block, model))
    front_pieces, gain_part, d_conv, u_low = then(front_pieces, gain_part, d_conv, u_low)

    gain_rows = jnp.pad(gain_part.reshape(parts, -1), ((0, 0), (0, block - gain.shape[0])))
    select_grad = mode_outer(d_proj, u_low, masks_t)
    cshift_grad = jnp.sum(d_conv, axis=(0, 1))
    conv_grad = jnp.stack(
        [jnp.sum(d_conv * extended[tap : tap + length], axis=(0, 1)) for tap in range(taps)]
    )
    grads = jnp.concatenate(
        [
            conv_grad,
            cshift_grad[None],
            sbias_grad,
            rate_grad,
            skip_grad[None],
            step_grad.reshape(copies * rank, width),
            select_grad.reshape(-1, width),
        ],
        axis=0,
    )
    grads = jnp.concatenate([in_order(grads, parts), gain_rows.reshape(1, width)], axis=0)
    other, front_pieces, grads = then(other, front_pieces, grads)
    own, sent = chips_sent(kept_part, other, low)
    rows_received = chips_received(sent)
    front_received = fsdp_received(front_pieces)
    sent, grads = then(sent, grads)
    grads = lax.psum_scatter(grads, "fsdp", scatter_dimension=1, tiled=True)
    gain_grad = grads[-1, : gain.shape[0]]

    front_even, front_odd = to_owners(
        jnp.swapaxes(summed(front_received).astype(low), 1, 2), 0
    )
    in_weight_grad = jnp.concatenate([gate_even + front_even, gate_odd + front_odd], axis=2).astype(full)
    d_rows = summed(own + rows_received)
    own = inputs.astype(full)
    own_inverse = lax.rsqrt(jnp.mean(own * own, axis=-1, keepdims=True) + epsilon)
    d_scaled = d_rows * gain_full
    input_grad = (
        out_grad.astype(full)
        + own_inverse * d_scaled
        - own * own_inverse**3 * jnp.mean(d_scaled * own, axis=-1, keepdims=True)
    )

    rows, at = [], 0
    for size in sizes[1:]:
        rows.append(grads[at : at + size])
        at += size
    return (
        output,
        input_grad,
        gain_grad,
        in_weight_grad,
        rows[0],
        rows[1][0],
        jnp.transpose(rows[6].reshape(copies, -1, block), (0, 2, 1)),
        rows[5].reshape(copies, rank, block),
        rows[2],
        rows[3],
        rows[4][0],
        out_weight_grad,
    )


def solution(mesh):
    whole = ("dp", "fsdp")
    return jax.shard_map(
        shards,
        mesh=mesh,
        in_specs=(
            P("dp", "fsdp", None),
            P("dp", "fsdp"),
            P(whole),
            P(None, None, whole),
            P(None, whole),
            P(whole),
            P(None, whole, None),
            P(None, None, whole),
            P(None, whole),
            P(None, whole),
            P(whole),
            P(None, whole, None),
            P("dp", "fsdp", None),
        ),
        out_specs=(
            P("dp", "fsdp", None),
            P("dp", "fsdp", None),
            P(whole),
            P(None, None, whole),
            P(None, whole),
            P(whole),
            P(None, whole, None),
            P(None, None, whole),
            P(None, whole),
            P(None, whole),
            P(whole),
            P(None, whole, None),
        ),
        check_vma=False,
    )
```

time: 5890 us -> 1300 us (0.22)
  waiting for transfers between devices: 4500 us -> 413 us
  blocking collectives: 401 us -> 149 us
  other arithmetic: 323 us -> 138 us
  Pallas kernels: 0 us -> 156 us
  matrix products: 349 us -> 201 us
  local copies, waits for them, and re-layouts: 266 us -> 139 us
  starting transfers between devices: 7.54 us -> 83.9 us
    reduce_scatter x5 -> x2, waiting for transfers between devices: 4040 us -> 0.02 us  [the longest x1 0.02 us: shards(): out_rows = lax.psum_scatter(out_sent, 'dp', scatter_dimension=0, tiled=True)]
    all_gather x7 -> x2, waiting for transfers between devices: 458 us -> 91.1 us  [the longest x1 91.1 us: shards(): lax.all_gather(inputs, 'dp', axis=0, tiled=True).reshape(tokens, model)]
    ppermute x2 -> x58, waiting for transfers between devices: 1.49 us -> 321 us  [the longest x48 235 us: exchanged(): lax.ppermute(value, axis, [(source, source ^ mask) for source in range(co...]
    all_gather x5 -> x1, blocking collectives: 315 us -> 80.5 us  [shards(): packed = in_order(lax.all_gather(packed, 'fsdp', axis=1, tiled=True), parts)]
    pallas_call x0 -> x4, Pallas kernels: none -> 156 us  [scan_call(): pl.pallas_call(kernel, grid=(count // SUB, steps), in_specs=[specs[name][...]
    dot_general x28 -> x16, matrix products: 347 us -> 201 us  [the longest x5 70.5 us: mode_dot(): lax.dot_general(masked(left, masks), weight, (((1, 2), (0, 1)), ((), ()))...]
    reduce_sum x235 -> x6, other arithmetic: 175 us -> 31.5 us  [the longest x1 14.1 us: shards(): gain_part = jnp.sum(d_normed * x_float * inverse, axis=0)]
    ppermute x2 -> x58, starting transfers between devices: 6.6 us -> 83.8 us  [the longest x48 53.9 us: exchanged(): lax.ppermute(value, axis, [(source, source ^ mask) for source in range(co...]
  transfers between devices with their start and end apart: 16 -> 62, of which waited for: 8 -> 23; matrix products, arithmetic and copies ran while one was open for 11% -> 27% of each run, Pallas kernels for 0% -> 9%
where the time goes in v1:
time: 1300 us
  waiting for transfers between devices  413 us (32%)
  matrix products  201 us (15%)
  Pallas kernels  156 us (12%)
  blocking collectives  149 us (11%)
  local copies, waits for them, and re-layouts  139 us (11%)
  other arithmetic  138 us (11%)
  starting transfers between devices  83.9 us (6%)
  between operations  17 us (1%)
    ppermute x48, waiting for transfers between devices, exchanged(): lax.ppermute(value, axis, [(source, source ^ mask) for source in range(co...  235 us
    pallas_call x4, Pallas kernels, scan_call(): pl.pallas_call(kernel, grid=(count // SUB, steps), in_specs=[specs[name][...  156 us
    all_gather x1, waiting for transfers between devices, shards(): lax.all_gather(inputs, 'dp', axis=0, tiled=True).reshape(tokens, model)  91.1 us
    ppermute x2, waiting for transfers between devices, to_owners(): lax.ppermute(piece, ('dp', 'fsdp'), [(2 * s + 1, first + s) for s in rang...  86.6 us
    all_gather x1, blocking collectives, shards(): packed = in_order(lax.all_gather(packed, 'fsdp', axis=1, tiled=True), parts)  80.5 us
    dot_general x5, matrix products, mode_dot(): lax.dot_general(masked(left, masks), weight, (((1, 2), (0, 1)), ((), ()))...  70.5 us
    unnamed x1, blocking collectives  68.9 us
    dot_general x5, matrix products, mode_dot_back(): lax.dot_general(masked(left, masks), weight, (((1, 2), (0, 2)), ((), ()))...  68.3 us
  transfers between devices with their start and end apart: 62, of which 23 were waited for; matrix products, arithmetic and copies ran while one was open for 27% of the time, Pallas kernels for 9%

profile of v1, /device:TPU:10, one launch (start us, length us, event | category | flops | bytes accessed | tf_op | source)
XLA Modules:
  0.0 1296.8 jit_solution(7310532829691458396)
XLA Ops:
  8.1 91.1 %all-gather.4.cloned.1.call-done = bf16[8,288,2048]{2,1,0:T(8,128)(2,1)} async-done(((bf16[1,288,2048]{2,1,0:T(8,128)(2,1)}), bf16[8,288,2048]{2,1,0:T(8,128)(2,1)}) %all-gather.4.cloned.1.call-update) | async-done | bytes 9437200 | tf_op jit(solution)/shard_map/all_gather | solution.py:436
  117.7 80.5 %all_gather.12 = bf16[890,512]{1,0:T(8,128)(2,1)S(1)} all-gather(bf16[890,128]{1,0:T(8,128)(2,1)S(1)} %concatenate.91), channel_id=1, replica_groups=mesh['dp'=8,'fsdp'=4] {'fsdp'}, dimensions={1}, use_global_device_ids=true | all-gather | bytes 1139200 | tf_op jit(solution)/shard_map/all_gather | solution.py:413
  200.1 68.9 %all-reduce.2 = bf16[4352]{0:T(1024)(128)(2,1)S(1)} all-reduce(bf16[4352]{0:T(1024)(128)(2,1)S(1)} %dynamic-update-slice), channel_id=2, replica_groups=mesh['dp'=8,'fsdp'=4] {'dp'}, use_global_device_ids=true, to_apply=%add.2 | all-reduce | flops 4352 | bytes 17408
  289.6 40.4 %collective-permute-done.4 = bf16[3,2048,128]{2,1,0:T(8,128)(2,1)S(1)} collective-permute-done((bf16[3,2048,128]{2,1,0:T(8,128)(2,1)S(1)}, bf16[3,2048,128]{2,1,0:T(8,128)(2,1)S(1)}, u32[]{:S(2)}, u32[]{:S(2)}) %collective-permute-start.4) | collective-permute-done | bytes 1572896 | tf_op jit(solution)/shard_map/ppermute | solution.py:266
  330.0 35.1 %collective-permute-done.3 = bf16[3,2048,128]{2,1,0:T(8,128)(2,1)S(1)} collective-permute-done((bf16[3,2048,128]{2,1,0:T(8,128)(2,1)S(1)}, bf16[3,2048,128]{2,1,0:T(8,128)(2,1)S(1)}, u32[]{:S(2)}, u32[]{:S(2)}) %collective-permute-start.3) | collective-permute-done | bytes 1572896 | tf_op jit(solution)/shard_map/ppermute | solution.py:266
  371.9 9.5 fusion.8
  381.4 19.4 %fusion.74 = bf16[2304,512]{1,0:T(8,128)(2,1)S(1)} fusion(bf16[2304,3]{0,1:T(4,128)(2,1)S(1)} %convert_convert_fusion.2, bf16[2304,2048]{1,0:T(8,128)(2,1)} %fusion.8, bf16[3,2048,512]{2,1,0:T(8,128)(2,1)} %pad_maximum_fusion.39), kind=kOutput, calls=%fused_computation.98 | convolution fusion | flops 14510850048 | bytes 18101760 | tf_op jit(solution)/shard_map/dot_general | solution.py:247
  428.3 21.3 %fusion.37 = f32[2304,512]{1,0:T(8,128)} fusion(bf16[3,512,2048]{2,1,0:T(8,128)(2,1)} %constant_dynamic-update-slice_fusion, bf16[2304,2048]{1,0:T(8,128)(2,1)} %bitcast.614, bf16[2304,3]{0,1:T(4,128)(2,1)S(1)} %convert_convert_fusion.2), kind=kOutput, calls=%fused_computation.47 | convolution fusion | flops 14509670400 | bytes 20461056 | tf_op jit(solution)/shard_map/dot_general | solution.py:253
  459.2 12.1 collective-permute-done.14
  493.2 7.7 collective-permute-done.16
  524.8 20.7 %shard_map.220 = (f32[16,8,512]{2,1,0:T(8,128)S(1)}, f32[8,512]{1,0:T(8,128)S(1)}) custom-call(f32[288,8,512]{2,1,0:T(8,128)S(1)} %get-tuple-element.414.d_ref, f32[288,8,512]{2,1,0:T(8,128)S(1)} %bitcast.512, bf16[1,2304,96]{2,1,0:T(8,128)(2,1)S(1)} %pad_maximum_fusion.16.parts_ref, bf16[96,4096]{1,0:T(8,128)(2,1)S(1)} %compare_convert_fusion.ones_ref, ...), custom_call_target="tpu_custom_call" | custom-call | flops 22649241600 | bytes 33030144 | tf_op jit(solution)/shard_map/pallas_call | solution.py:225
  559.7 19.6 %fusion.71 = bf16[2304,512]{1,0:T(8,128)(2,1)S(1)} fusion(bf16[3,2048,512]{2,1,0:T(8,128)(2,1)} %constant_dynamic-update-slice_fusion.4, bf16[2304,2048]{1,0:T(8,128)(2,1)} %fusion.8, bf16[2304,3]{0,1:T(4,128)(2,1)S(1)} %copy-done.70), kind=kOutput, calls=%fused_computation.97 | convolution fusion | flops 14510850048 | bytes 18101760 | tf_op jit(solution)/shard_map/dot_general | solution.py:247
  581.3 9.9 multiply_reduce_fusion.4
  591.3 19.6 %shard_map.221.refs_0_ = f32[16,8,512]{2,1,0:T(8,128)S(1)} custom-call(f32[288,8,512]{2,1,0:T(8,128)S(1)} %bitcast.521, f32[288,8,512]{2,1,0:T(8,128)S(1)} %get-tuple-element.261.y_ref, bf16[1,2304,96]{2,1,0:T(8,128)(2,1)S(1)} %pad_maximum_fusion.16.parts_ref, bf16[96,4096]{1,0:T(8,128)(2,1)S(1)} %compare_convert_fusion.ones_ref, ...), custom_call_target="tpu_custom_call" | custom-call | flops 22649241600 | bytes 28311552 | tf_op jit(solution)/shard_map/pallas_call | solution.py:225
  615.9 30.1 %shard_map.222 = (f32[288,8,512]{2,1,0:T(8,128)S(1)}, f32[18,16,8,512]{3,2,1,0:T(8,128)S(1)}) custom-call(f32[288,8,512]{2,1,0:T(8,128)} %copy-done.8, f32[288,8,512]{2,1,0:T(8,128)} %get-tuple-element.265.u_ref, bf16[1,2304,96]{2,1,0:T(8,128)(2,1)S(1)} %pad_maximum_fusion.16.parts_ref, bf16[96,4096]{1,0:T(8,128)(2,1)S(1)} %compare_convert_fusion.ones_ref, ...), custom_call_target="tpu_custom_call" | custom-call | flops 33973862400 | bytes 37748736 | tf_op jit(solution)/shard_map/pallas_call | solution.py:225
  646.3 10.4 fusion.107
  663.2 17.8 %fusion.19 = f32[3,512,2048]{2,1,0:T(8,128)S(1)} fusion(bf16[2304,2048]{1,0:T(8,128)(2,1)} %fusion.8, bf16[2304,3]{0,1:T(4,128)(2,1)S(1)} %copy-done.71, bf16[2304,512]{0,1:T(8,128)(2,1)} %copy.123), kind=kOutput, calls=%fused_computation.27 | convolution fusion | flops 14499053568 | bytes 24393216 | tf_op jit(solution)/shard_map/dot_general | solution.py:259
  691.8 20.4 %bitcast_convert_fusion = bf16[2304,2048]{1,0:T(8,128)(2,1)} fusion(bf16[3,512,2048]{2,1,0:T(8,128)(2,1)} %constant_dynamic-update-slice_fusion, bf16[2304,512]{0,1:T(8,128)(2,1)} %copy.127, bf16[2304,3]{0,1:T(4,128)(2,1)S(1)} %copy-done.71), kind=kOutput, calls=%fused_computation.15 | convolution fusion | flops 14503772160 | bytes 18101760 | tf_op jit(solution)/shard_map/dot_general | solution.py:247
  720.1 19.7 %fusion.188 = (bf16[3,4,128,2048]{3,2,0,1:T(8,128)(2,1)S(1)}, f32[3,4,128,2048]{3,2,0,1:T(8,128)}) fusion(bf16[2304,2048,1,1]{1,0,2,3:T(8,128)(2,1)} %bitcast.615, bf16[3,2304]{1,0:T(4,128)(2,1)S(1)} %copy-done.73, bf16[4,128,2304]{2,1,0:T(8,128)(2,1)} %bitcast.558), kind=kOutput, calls=%fused_computation.420 | convolution fusion | flops 14502199296 | bytes 30684672 | tf_op jit(solution)/shard_map/dot_general | solution.py:259
  743.3 10.9 collective-permute-done.28
  756.0 85.2 %shard_map.223 = (f32[288,8,512]{2,1,0:T(8,128)S(1)}, f32[288,8,512]{2,1,0:T(8,128)}, f32[288,8,32]{2,1,0:T(8,128)S(1)}, f32[16,8,512]{2,1,0:T(8,128)S(1)}) custom-call(f32[288,8,512]{2,1,0:T(8,128)} %copy-done.8, f32[288,8,512]{2,1,0:T(8,128)} %get-tuple-element.265.u_ref, f32[288,8,512]{2,1,0:T(8,128)} %copy-done, bf16[1,2304,96]{2,1,0:T(8,128)(2,1)S(1)} %copy-done.3, ...), custom_call_target="tpu_custom_call" | custom-call | flops 90596966400 | bytes 56623104 | tf_op jit(solution)/shard_map/pallas_call | solution.py:225
  878.1 20.6 %convolution_bitcast_fusion = f32[2304,2048]{1,0:T(8,128)} fusion(bf16[3,2048,512]{2,1,0:T(8,128)(2,1)} %constant_dynamic-update-slice_fusion.4, bf16[2304,512]{0,1:T(8,128)(2,1)} %copy.135, bf16[2304,3]{0,1:T(4,128)(2,1)S(1)} %copy-done.72), kind=kOutput, calls=%fused_computation.23 | convolution fusion | flops 14499053568 | bytes 27538944 | tf_op jit(solution)/shard_map/dot_general | solution.py:253
  907.3 9.2 collective-permute-done.37
  960.9 7.7 fusion.114
  971.8 20.4 %fusion.25 = f32[2304,2048,1]{1,0,2:T(8,128)} fusion(bf16[2304,512]{0,1:T(8,128)(2,1)} %copy.142, bf16[2304,3]{0,1:T(4,128)(2,1)S(1)} %copy-done.72, bf16[3,2048,128]{2,1,0:T(8,128)(2,1)} %copy-done.38, bf16[3,2048,128]{2,1,0:T(8,128)(2,1)} %copy-done.39, bf16[3,2048,128]{2,1,0:T(8,128)(2,1)} %copy-done.40, bf16[3,2048,128]{2,1,0:T(8,128)(2,1)} %copy-done.31), kind=kOutput, calls=%fused_computation.33 | convolution fusion | flops 14524219392 | bytes 27538944 | tf_op jit(solution)/shard_map/dot_general | solution.py:253
  992.3 14.1 %fusion.10 = (f32[2048]{0:T(1024)S(1)}, bf16[2304,2048]{1,0:T(8,128)(2,1)S(1)}) fusion(bf16[2304,2048]{1,0:T(8,128)(2,1)S(1)} %bitcast.530, f32[2304]{0:T(1024)S(1)} %copy-done.61, f32[2304,2048]{1,0:T(8,128)} %convolution_bitcast_fusion, f32[2304,2048,1]{1,0,2:T(8,128)} %fusion.25), kind=kLoop, calls=%fused_computation.13 | loop fusion | flops 28309504 | bytes 56640512 | tf_op jit(solution)/shard_map/reduce_sum | solution.py:596
  1006.4 22.2 %collective-permute-done.44 = bf16[3,2048,128]{1,2,0:T(8,128)(2,1)} collective-permute-done((bf16[3,2048,128]{1,2,0:T(8,128)(2,1)}, bf16[3,2048,128]{1,2,0:T(8,128)(2,1)}, u32[]{:S(2)}, u32[]{:S(2)}) %collective-permute-start.44) | collective-permute-done | bytes 1572896 | tf_op jit(solution)/shard_map/ppermute | solution.py:342
  1033.5 19.7 %fusion.17 = f32[3,512,2048]{2,1,0:T(8,128)} fusion(bf16[2304,2048]{1,0:T(8,128)(2,1)} %fusion.8, bf16[2304,512]{0,1:T(8,128)(2,1)} %copy.145, bf16[2304,3]{0,1:T(4,128)(2,1)S(1)} %copy-done.72), kind=kOutput, calls=%fused_computation.25 | convolution fusion | flops 14499053568 | bytes 24393216 | tf_op jit(solution)/shard_map/dot_general | solution.py:259
  1097.4 28.5 %collective-permute-done.55 = bf16[3,128,2048]{2,1,0:T(8,128)(2,1)} collective-permute-done((bf16[3,128,2048]{2,1,0:T(8,128)(2,1)}, bf16[3,128,2048]{2,1,0:T(8,128)(2,1)}, u32[]{:S(2)}, u32[]{:S(2)}) %collective-permute-start.55) | collective-permute-done | bytes 1572896 | tf_op jit(solution)/shard_map/ppermute | solution.py:266
  1131.1 34.3 %collective-permute-done.54 = bf16[3,128,2048]{2,1,0:T(8,128)(2,1)} collective-permute-done((bf16[3,128,2048]{2,1,0:T(8,128)(2,1)}, bf16[3,128,2048]{2,1,0:T(8,128)(2,1)}, u32[]{:S(2)}, u32[]{:S(2)}) %collective-permute-start.54) | collective-permute-done | bytes 1572896 | tf_op jit(solution)/shard_map/ppermute | solution.py:266
  1173.4 23.6 %collective-permute-done.51 = bf16[1,288,2048]{2,1,0:T(8,128)(2,1)S(1)} collective-permute-done((bf16[1,288,2048]{2,1,0:T(8,128)(2,1)}, bf16[1,288,2048]{2,1,0:T(8,128)(2,1)S(1)}, u32[]{:S(2)}, u32[]{:S(2)}) %collective-permute-start.51) | collective-permute-done | bytes 1179680 | tf_op jit(solution)/shard_map/ppermute | solution.py:266
  1202.0 64.4 %collective-permute-done.57 = bf16[3,2048,128]{1,2,0:T(8,128)(2,1)S(1)} collective-permute-done((bf16[3,2048,128]{1,2,0:T(8,128)(2,1)S(1)}, bf16[3,2048,128]{1,2,0:T(8,128)(2,1)S(1)}, u32[]{:S(2)}, u32[]{:S(2)}) %collective-permute-start.57) | collective-permute-done | bytes 1572896 | tf_op jit(solution)/shard_map/ppermute | solution.py:342
  (550 shorter events, 365.0 us)
Async XLA Ops:
  7.3 91.9 %all-gather.4.cloned.1.call-start = ((), (), s32[]{:S(2)}) async-start(), calls=%async_computation.2 | async-start | bytes 10616832 | tf_op jit(solution)/shard_map/all_gather | solution.py:436
  8.0 415.3 %all-gather.6.cloned.1.call-start = ((), (), s32[]{:S(2)}) async-start(), calls=%async_computation.3 | async-start | bytes 10616832 | tf_op jit(solution)/shard_map/all_gather | solution.py:442
  99.2 839.0 %reduce-scatter.3.cloned.1.call-start = ((), (), s32[]{:S(2)}) async-start(), calls=%async_computation.4 | async-start | bytes 10616832 | tf_op jit(solution)/shard_map/reduce_scatter | solution.py:544
  99.2 180.7 %collective-permute-start.6 = (bf16[3,128,2048]{2,1,0:T(8,128)(2,1)}, bf16[3,128,2048]{2,1,0:T(8,128)(2,1)}, u32[]{:S(2)}, u32[]{:S(2)}) collective-permute-start(bf16[3,128,2048]{2,1,0:T(8,128)(2,1)} %param.24), channel_id=1, source_target_pairs={{0,1},{1,0},{2,3},{3,2},{4,5},{5,4},{6,7},{7,6},{8,9},{9,8},{10,11... | collective-permute-start | bytes 4718600 | tf_op jit(solution)/shard_map/ppermute | solution.py:266
  99.6 182.0 %collective-permute-start.7 = (bf16[3,128,2048]{2,1,0:T(8,128)(2,1)}, bf16[3,128,2048]{2,1,0:T(8,128)(2,1)}, u32[]{:S(2)}, u32[]{:S(2)}) collective-permute-start(bf16[3,128,2048]{2,1,0:T(8,128)(2,1)} %param.24), channel_id=1, source_target_pairs={{0,2},{1,3},{2,0},{3,1},{4,6},{5,7},{6,4},{7,5},{8,10},{9,11},{10,... | collective-permute-start | bytes 4718600 | tf_op jit(solution)/shard_map/ppermute | solution.py:266
  101.3 180.3 %collective-permute-start.8 = (bf16[3,128,2048]{2,1,0:T(8,128)(2,1)}, bf16[3,128,2048]{2,1,0:T(8,128)(2,1)}, u32[]{:S(2)}, u32[]{:S(2)}) collective-permute-start(bf16[3,128,2048]{2,1,0:T(8,128)(2,1)} %param.24), channel_id=1, source_target_pairs={{0,3},{1,2},{2,1},{3,0},{4,7},{5,6},{6,5},{7,4},{8,11},{9,10},{10,... | collective-permute-start | bytes 4718600 | tf_op jit(solution)/shard_map/ppermute | solution.py:266
  106.5 169.1 %collective-permute-start = (bf16[3,2048,128]{2,1,0:T(8,128)(2,1)}, bf16[3,2048,128]{2,1,0:T(8,128)(2,1)}, u32[]{:S(2)}, u32[]{:S(2)}) collective-permute-start(bf16[3,2048,128]{2,1,0:T(8,128)(2,1)} %get-tuple-element.286), channel_id=1, source_target_pairs={{0,0},{1,2},{2,4},{3,6},{4,8},{5,10},{6,12},{7,14},{8,16},{9,18},{... | collective-permute-start | bytes 4718600 | tf_op jit(solution)/shard_map/ppermute | solution.py:334
  113.1 162.5 %collective-permute-start.1 = (bf16[3,2048,128]{2,1,0:T(8,128)(2,1)}, bf16[3,2048,128]{2,1,0:T(8,128)(2,1)}, u32[]{:S(2)}, u32[]{:S(2)}) collective-permute-start(bf16[3,2048,128]{2,1,0:T(8,128)(2,1)} %get-tuple-element.285), channel_id=1, source_target_pairs={{0,1},{1,3},{2,5},{3,7},{4,9},{5,11},{6,13},{7,15},{8,17},{9,19},{... | collective-permute-start | bytes 4718600 | tf_op jit(solution)/shard_map/ppermute | solution.py:335
  278.0 52.0 %collective-permute-start.4 = (bf16[3,2048,128]{2,1,0:T(8,128)(2,1)S(1)}, bf16[3,2048,128]{2,1,0:T(8,128)(2,1)S(1)}, u32[]{:S(2)}, u32[]{:S(2)}) collective-permute-start(bf16[3,2048,128]{2,1,0:T(8,128)(2,1)S(1)} %add.361), channel_id=1, source_target_pairs={{0,3},{1,2},{2,1},{3,0},{4,7},{5,6},{6,5},{7,4},{8,11},{9,10},{10,... | collective-permute-start | bytes 4718600 | tf_op jit(solution)/shard_map/ppermute | solution.py:266
  278.3 86.8 %collective-permute-start.3 = (bf16[3,2048,128]{2,1,0:T(8,128)(2,1)S(1)}, bf16[3,2048,128]{2,1,0:T(8,128)(2,1)S(1)}, u32[]{:S(2)}, u32[]{:S(2)}) collective-permute-start(bf16[3,2048,128]{2,1,0:T(8,128)(2,1)S(1)} %add.361), channel_id=1, source_target_pairs={{0,2},{1,3},{2,0},{3,1},{4,6},{5,7},{6,4},{7,5},{8,10},{9,11},{10,... | collective-permute-start | bytes 4718600 | tf_op jit(solution)/shard_map/ppermute | solution.py:266
  279.9 85.3 %collective-permute-start.2 = (bf16[3,2048,128]{2,1,0:T(8,128)(2,1)S(1)}, bf16[3,2048,128]{2,1,0:T(8,128)(2,1)S(1)}, u32[]{:S(2)}, u32[]{:S(2)}) collective-permute-start(bf16[3,2048,128]{2,1,0:T(8,128)(2,1)S(1)} %add.361), channel_id=1, source_target_pairs={{0,1},{1,0},{2,3},{3,2},{4,5},{5,4},{6,7},{7,6},{8,9},{9,8},{10,11... | collective-permute-start | bytes 4718600 | tf_op jit(solution)/shard_map/ppermute | solution.py:266
  283.8 124.3 %collective-permute-start.9 = (bf16[3,2048,128]{2,1,0:T(8,128)(2,1)}, bf16[3,2048,128]{2,1,0:T(8,128)(2,1)S(1)}, u32[]{:S(2)}, u32[]{:S(2)}) collective-permute-start(bf16[3,2048,128]{2,1,0:T(8,128)(2,1)} %get-tuple-element.284), channel_id=1, source_target_pairs={{16,0},{17,2},{18,4},{19,6},{20,8},{21,10},{22,12},{23,14},{24,16}... | collective-permute-start | bytes 4718600 | tf_op jit(solution)/shard_map/ppermute | solution.py:334
  284.6 123.5 %collective-permute-start.10 = (bf16[3,2048,128]{2,1,0:T(8,128)(2,1)}, bf16[3,2048,128]{2,1,0:T(8,128)(2,1)S(1)}, u32[]{:S(2)}, u32[]{:S(2)}) collective-permute-start(bf16[3,2048,128]{2,1,0:T(8,128)(2,1)} %get-tuple-element.283), channel_id=1, source_target_pairs={{16,1},{17,3},{18,5},{19,7},{20,9},{21,11},{22,13},{23,15},{24,17}... | collective-permute-start | bytes 4718600 | tf_op jit(solution)/shard_map/ppermute | solution.py:335
  409.8 74.2 %collective-permute-start.18 = (bf16[3,2048,128]{2,1,0:T(8,128)(2,1)}, bf16[3,2048,128]{2,1,0:T(8,128)(2,1)}, u32[]{:S(2)}, u32[]{:S(2)}) collective-permute-start(bf16[3,2048,128]{2,1,0:T(8,128)(2,1)} %add.362), channel_id=1, source_target_pairs={{0,1},{1,0},{2,3},{3,2},{4,5},{5,4},{6,7},{7,6},{8,9},{9,8},{10,11... | collective-permute-start | bytes 4718600 | tf_op jit(solution)/shard_map/ppermute | solution.py:266
  410.8 76.5 %collective-permute-start.19 = (bf16[3,2048,128]{2,1,0:T(8,128)(2,1)}, bf16[3,2048,128]{2,1,0:T(8,128)(2,1)}, u32[]{:S(2)}, u32[]{:S(2)}) collective-permute-start(bf16[3,2048,128]{2,1,0:T(8,128)(2,1)} %add.362), channel_id=1, source_target_pairs={{0,2},{1,3},{2,0},{3,1},{4,6},{5,7},{6,4},{7,5},{8,10},{9,11},{10,... | collective-permute-start | bytes 4718600 | tf_op jit(solution)/shard_map/ppermute | solution.py:266
  412.3 75.0 %collective-permute-start.20 = (bf16[3,2048,128]{2,1,0:T(8,128)(2,1)}, bf16[3,2048,128]{2,1,0:T(8,128)(2,1)}, u32[]{:S(2)}, u32[]{:S(2)}) collective-permute-start(bf16[3,2048,128]{2,1,0:T(8,128)(2,1)} %add.362), channel_id=1, source_target_pairs={{0,3},{1,2},{2,1},{3,0},{4,7},{5,6},{6,5},{7,4},{8,11},{9,10},{10,... | collective-permute-start | bytes 4718600 | tf_op jit(solution)/shard_map/ppermute | solution.py:266
  717.5 130.0 %collective-permute-start.29 = (bf16[3,128,2048]{2,1,0:T(8,128)(2,1)}, bf16[3,128,2048]{2,1,0:T(8,128)(2,1)}, u32[]{:S(2)}, u32[]{:S(2)}) collective-permute-start(bf16[3,128,2048]{2,1,0:T(8,128)(2,1)} %get-tuple-element.157), channel_id=1, source_target_pairs={{0,2},{1,3},{2,0},{3,1},{4,6},{5,7},{6,4},{7,5},{8,10},{9,11},{10,... | collective-permute-start | bytes 4718600 | tf_op jit(solution)/shard_map/ppermute | solution.py:266
  718.9 128.6 %collective-permute-start.30 = (bf16[3,128,2048]{2,1,0:T(8,128)(2,1)S(1)}, bf16[3,128,2048]{2,1,0:T(8,128)(2,1)}, u32[]{:S(2)}, u32[]{:S(2)}) collective-permute-start(bf16[3,128,2048]{2,1,0:T(8,128)(2,1)S(1)} %get-tuple-element.149.refs_1_), channel_id=1, source_target_pairs={{0,3},{1,2},{2,1},{3,0},{4,7},{5,6},{6,5},{7,4},{8,11},{9,10},{10,... | collective-permute-start | bytes 4718600 | tf_op jit(solution)/shard_map/ppermute | solution.py:266
  720.0 560.5 %reduce-scatter.5.cloned.1.call-start = ((), (), s32[]{:S(2)}) async-start(), calls=%async_computation.5 | async-start | bytes 2293760 | tf_op jit(solution)/shard_map/reduce_scatter | solution.py:628
  740.5 107.0 %collective-permute-start.31 = (bf16[3,128,2048]{2,1,0:T(8,128)(2,1)S(1)}, bf16[3,128,2048]{2,1,0:T(8,128)(2,1)S(1)}, u32[]{:S(2)}, u32[]{:S(2)}) collective-permute-start(bf16[3,128,2048]{2,1,0:T(8,128)(2,1)S(1)} %get-tuple-element.278), channel_id=1, source_target_pairs={{0,1},{1,0},{2,3},{3,2},{4,5},{5,4},{6,7},{7,6},{8,9},{9,8},{10,11... | collective-permute-start | bytes 4718600 | tf_op jit(solution)/shard_map/ppermute | solution.py:266
  741.6 111.7 %collective-permute-start.32 = (bf16[3,128,2048]{2,1,0:T(8,128)(2,1)S(1)}, bf16[3,128,2048]{2,1,0:T(8,128)(2,1)S(1)}, u32[]{:S(2)}, u32[]{:S(2)}) collective-permute-start(bf16[3,128,2048]{2,1,0:T(8,128)(2,1)S(1)} %get-tuple-element.277), channel_id=1, source_target_pairs={{0,2},{1,3},{2,0},{3,1},{4,6},{5,7},{6,4},{7,5},{8,10},{9,11},{10,... | collective-permute-start | bytes 4718600 | tf_op jit(solution)/shard_map/ppermute | solution.py:266
  754.2 99.2 %collective-permute-start.33 = (bf16[3,128,2048]{2,1,0:T(8,128)(2,1)S(1)}, bf16[3,128,2048]{2,1,0:T(8,128)(2,1)S(1)}, u32[]{:S(2)}, u32[]{:S(2)}) collective-permute-start(bf16[3,128,2048]{2,1,0:T(8,128)(2,1)S(1)} %get-tuple-element.279.refs_2_), channel_id=1, source_target_pairs={{0,3},{1,2},{2,1},{3,0},{4,7},{5,6},{6,5},{7,4},{8,11},{9,10},{10,... | collective-permute-start | bytes 4718600 | tf_op jit(solution)/shard_map/ppermute | solution.py:266
  951.6 54.7 %collective-permute-start.43 = (bf16[3,2048,128]{1,2,0:T(8,128)(2,1)}, bf16[3,2048,128]{1,2,0:T(8,128)(2,1)}, u32[]{:S(2)}, u32[]{:S(2)}) collective-permute-start(bf16[3,2048,128]{1,2,0:T(8,128)(2,1)} %fusion.119), channel_id=1, source_target_pairs={{0,16},{2,17},{4,18},{6,19},{8,20},{10,21},{12,22},{14,23},{16,24}... | collective-permute-start | bytes 4718600 | tf_op jit(solution)/shard_map/ppermute | solution.py:341
  953.4 75.1 %collective-permute-start.44 = (bf16[3,2048,128]{1,2,0:T(8,128)(2,1)}, bf16[3,2048,128]{1,2,0:T(8,128)(2,1)}, u32[]{:S(2)}, u32[]{:S(2)}) collective-permute-start(bf16[3,2048,128]{1,2,0:T(8,128)(2,1)} %fusion.119), channel_id=1, source_target_pairs={{1,16},{3,17},{5,18},{7,19},{9,20},{11,21},{13,22},{15,23},{17,24}... | collective-permute-start | bytes 4718600 | tf_op jit(solution)/shard_map/ppermute | solution.py:342
  1031.0 48.9 %collective-permute-start.45 = (bf16[4,1,288,2048]{3,2,1,0:T(8,128)(2,1)}, bf16[4,1,288,2048]{3,2,1,0:T(8,128)(2,1)}, u32[]{:S(2)}, u32[]{:S(2)}) collective-permute-start(bf16[4,1,288,2048]{3,2,1,0:T(8,128)(2,1)} %dynamic-slice_bitcast_fusion), channel_id=1, source_target_pairs={{0,4},{4,0},{8,12},{12,8},{16,20},{20,16},{24,28},{28,24},{1,5},{5... | collective-permute-start | bytes 14155784 | tf_op jit(solution)/shard_map/ppermute | solution.py:266
  1082.2 83.3 %collective-permute-start.54 = (bf16[3,128,2048]{2,1,0:T(8,128)(2,1)}, bf16[3,128,2048]{2,1,0:T(8,128)(2,1)}, u32[]{:S(2)}, u32[]{:S(2)}) collective-permute-start(bf16[3,128,2048]{2,1,0:T(8,128)(2,1)} %get-tuple-element.193), channel_id=1, source_target_pairs={{0,2},{1,3},{2,0},{3,1},{4,6},{5,7},{6,4},{7,5},{8,10},{9,11},{10,... | collective-permute-start | bytes 4718600 | tf_op jit(solution)/shard_map/ppermute | solution.py:266
  1082.8 82.6 %collective-permute-start.53 = (bf16[3,128,2048]{2,1,0:T(8,128)(2,1)}, bf16[3,128,2048]{2,1,0:T(8,128)(2,1)}, u32[]{:S(2)}, u32[]{:S(2)}) collective-permute-start(bf16[3,128,2048]{2,1,0:T(8,128)(2,1)} %get-tuple-element.192), channel_id=1, source_target_pairs={{0,1},{1,0},{2,3},{3,2},{4,5},{5,4},{6,7},{7,6},{8,9},{9,8},{10,11... | collective-permute-start | bytes 4718600 | tf_op jit(solution)/shard_map/ppermute | solution.py:266
  1095.0 78.5 %collective-permute-start.52 = (bf16[1,288,2048]{2,1,0:T(8,128)(2,1)}, bf16[1,288,2048]{2,1,0:T(8,128)(2,1)S(1)}, u32[]{:S(2)}, u32[]{:S(2)}) collective-permute-start(bf16[1,288,2048]{2,1,0:T(8,128)(2,1)} %get-tuple-element.272), channel_id=1, source_target_pairs={{0,24},{4,28},{8,16},{12,20},{16,8},{20,12},{24,0},{28,4},{1,25},{... | collective-permute-start | bytes 3538952 | tf_op jit(solution)/shard_map/ppermute | solution.py:266
  1096.4 100.7 %collective-permute-start.51 = (bf16[1,288,2048]{2,1,0:T(8,128)(2,1)}, bf16[1,288,2048]{2,1,0:T(8,128)(2,1)S(1)}, u32[]{:S(2)}, u32[]{:S(2)}) collective-permute-start(bf16[1,288,2048]{2,1,0:T(8,128)(2,1)} %get-tuple-element.273), channel_id=1, source_target_pairs={{0,16},{4,20},{8,24},{12,28},{16,0},{20,4},{24,8},{28,12},{1,17},{... | collective-permute-start | bytes 3538952 | tf_op jit(solution)/shard_map/ppermute | solution.py:266
  1125.9 71.1 %collective-permute-start.50 = (bf16[1,288,2048]{2,1,0:T(8,128)(2,1)}, bf16[1,288,2048]{2,1,0:T(8,128)(2,1)S(1)}, u32[]{:S(2)}, u32[]{:S(2)}) collective-permute-start(bf16[1,288,2048]{2,1,0:T(8,128)(2,1)} %get-tuple-element.271), channel_id=1, source_target_pairs={{0,8},{4,12},{8,0},{12,4},{16,24},{20,28},{24,16},{28,20},{1,9},{5... | collective-permute-start | bytes 3538952 | tf_op jit(solution)/shard_map/ppermute | solution.py:266
  1169.0 97.5 %collective-permute-start.57 = (bf16[3,2048,128]{1,2,0:T(8,128)(2,1)S(1)}, bf16[3,2048,128]{1,2,0:T(8,128)(2,1)S(1)}, u32[]{:S(2)}, u32[]{:S(2)}) collective-permute-start(bf16[3,2048,128]{1,2,0:T(8,128)(2,1)S(1)} %fusion.120), channel_id=1, source_target_pairs={{1,0},{3,1},{5,2},{7,3},{9,4},{11,5},{13,6},{15,7},{17,8},{19,9},{... | collective-permute-start | bytes 4718600 | tf_op jit(solution)/shard_map/ppermute | solution.py:342
  1171.5 97.0 %collective-permute-start.56 = (bf16[3,2048,128]{1,2,0:T(8,128)(2,1)S(1)}, bf16[3,2048,128]{1,2,0:T(8,128)(2,1)S(1)}, u32[]{:S(2)}, u32[]{:S(2)}) collective-permute-start(bf16[3,2048,128]{1,2,0:T(8,128)(2,1)S(1)} %fusion.120), channel_id=1, source_target_pairs={{0,0},{2,1},{4,2},{6,3},{8,4},{10,5},{12,6},{14,7},{16,8},{18,9},{... | collective-permute-start | bytes 4718600 | tf_op jit(solution)/shard_map/ppermute | solution.py:341
  (147 other events, 4933.8 us)
Sparse Core Ops, SparseCore 0:
  9.7 89.3 all-gather.3
  100.8 124.1 all-gather.5
  720.1 95.2 reduce-scatter.2
  1095.1 61.5 reduce-scatter.4

commit v2 on v1

--- a/solution.py
+++ b/solution.py
@@ -49,7 +49,7 @@
             d, u = d_ref[t, :, lanes], u_ref[t, :, lanes]
             return jnp.exp2(d[None] * rate) * state + (d * u)[None] * spread[t, :states]
 
-        end_ref[:, :, lanes] = lax.fori_loop(0, chunk, body, end_ref[:, :, lanes], unroll=4)
+        end_ref[:, :, lanes] = lax.fori_loop(0, chunk, body, end_ref[:, :, lanes], unroll=8)
 
 
 def ahead_kernel(d_ref, y_ref, parts_ref, ones_ref, rate_ref, out_ref, spread):
@@ -67,7 +67,7 @@
             d, dy = d_ref[t, :, lanes], y_ref[t, :, lanes]
             return jnp.exp2(d[None] * rate) * (grad + dy[None] * spread[t, states:])
 
-        out_ref[:, :, lanes] = lax.fori_loop(0, chunk, body, out_ref[:, :, lanes], unroll=4)
+        out_ref[:, :, lanes] = lax.fori_loop(0, chunk, body, out_ref[:, :, lanes], unroll=8)
 
 
 def forward_kernel(
@@ -91,7 +91,7 @@
             y_ref[t, :, lanes] = jnp.sum(state * spread[t, states:], axis=0)
             return state
 
-        state_ref[:, :, lanes] = lax.fori_loop(0, chunk, body, state_ref[:, :, lanes], unroll=4)
+        state_ref[:, :, lanes] = lax.fori_loop(0, chunk, body, state_ref[:, :, lanes], unroll=8)
 
 
 def backward_kernel(
@@ -128,7 +128,7 @@
                 held[t + 1] = state
                 return state
 
-            lax.fori_loop(0, chunk, forward, held[0], unroll=4)
+            lax.fori_loop(0, chunk, forward, held[0], unroll=8)
 
             def backward(k, carry):
                 t = chunk - 1 - k
@@ -160,7 +160,7 @@
                 chunk,
                 backward,
                 (grad_ref[low:high, :, lanes], drate_ref[low:high, :, lanes]),
-                unroll=4,
+                unroll=8,
             )
             grad_ref[low:high, :, lanes] = ahead
             drate_ref[low:high, :, lanes] = drate
@@ -174,7 +174,7 @@
         dmaps_ref[t] = total[:, : 2 * states]
         return 0
 
-    lax.fori_loop(0, chunk, gather, 0, unroll=4)
+    lax.fori_loop(0, chunk, gather, 0, unroll=8)
 
 
 def scan_call(kernel, delta, states, reverse, ins, outs, scratch, cost, after=()):
@@ -261,6 +261,81 @@
     )
 
 
+def outer_kernel(left_ref, right_ref, masks_ref, own_ref, *other_refs):
+    block = own_ref.shape[1]
+    for k in range(own_ref.shape[0]):
+        total = jnp.dot(
+            left_ref[...] * masks_ref[k : k + 1, :],
+            right_ref[...],
+            preferred_element_type=jnp.float32,
+        )
+        own_ref[k] = total[:block]
+        for m, other_ref in enumerate(other_refs):
+            other_ref[k] = total[(m + 1) * block : (m + 2) * block].astype(jnp.bfloat16)
+
+
+def outer_pieces(left, right, masks, parts):
+    width, tokens = left.shape
+    columns, copies = right.shape[1], masks.shape[0]
+    block, tile = width // parts, math.gcd(columns, 512)
+    kinds = [jnp.float32] + [jnp.bfloat16] * (parts - 1)
+    return pl.pallas_call(
+        outer_kernel,
+        grid=(columns // tile,),
+        in_specs=[
+            pl.BlockSpec((width, tokens), lambda n: (0, 0)),
+            pl.BlockSpec((tokens, tile), lambda n: (0, n)),
+            pl.BlockSpec((copies, tokens), lambda n: (0, 0)),
+        ],
+        out_specs=[pl.BlockSpec((copies, block, tile), lambda n: (0, 0, n))] * parts,
+        out_shape=[jax.ShapeDtypeStruct((copies, block, columns), kind) for kind in kinds],
+        compiler_params=pltpu.CompilerParams(vmem_limit_bytes=56 * 1024 * 1024),
+        cost_estimate=pl.CostEstimate(flops=1000, bytes_accessed=1000, transcendentals=0),
+    )(left, right, masks)
+
+
+def back_kernel(left_ref, weight_ref, base_ref, out_ref):
+    rows = math.gcd(left_ref.shape[1], 384)
+
+    def body(i, _):
+        at = pl.ds(pl.multiple_of(i * rows, rows), rows)
+        total = base_ref[at, :]
+        for k in range(left_ref.shape[0]):
+            total = total + lax.dot_general(
+                left_ref[k, at, :],
+                weight_ref[k],
+                (((1,), (1,)), ((), ())),
+                preferred_element_type=jnp.float32,
+            )
+        out_ref[at, :] = total.astype(jnp.bfloat16)
+        return 0
+
+    lax.fori_loop(0, left_ref.shape[1] // rows, body, 0)
+
+
+def product_back(left, weight, base):
+    copies, tokens, width = left.shape
+    columns = weight.shape[1]
+    tile = math.gcd(columns, 512)
+    return pl.pallas_call(
+        back_kernel,
+        grid=(columns // tile,),
+        in_specs=[
+            pl.BlockSpec((copies, tokens, width), lambda n: (0, 0, 0)),
+            pl.BlockSpec((copies, tile, width), lambda n: (0, n, 0)),
+            pl.BlockSpec((tokens, tile), lambda n: (0, n)),
+        ],
+        out_specs=pl.BlockSpec((tokens, tile), lambda n: (0, n)),
+        out_shape=jax.ShapeDtypeStruct((tokens, columns), jnp.bfloat16),
+        compiler_params=pltpu.CompilerParams(vmem_limit_bytes=56 * 1024 * 1024),
+        cost_estimate=pl.CostEstimate(
+            flops=2 * copies * tokens * columns * width,
+            bytes_accessed=6 * tokens * columns,
+            transcendentals=0,
+        ),
+    )(left, weight, base)
+
+
 def exchanged(value, axis, mask):
     count = lax.axis_size(axis)
     return lax.ppermute(value, axis, [(source, source ^ mask) for source in range(count)])
@@ -327,20 +402,33 @@
     return jnp.concatenate([piece_of(pieces, here ^ k) for k in range(blocks)], axis=-1)
 
 
-def to_workers(block, first):
+def moved(one, two, back):
+    half = lax.axis_size("dp") * lax.axis_size("fsdp") // 2
+    first = [(s, 2 * s) for s in range(half)] + [(half + s, 2 * s + 1) for s in range(half)]
+    second = [(s, 2 * s + 1) for s in range(half)] + [(half + s, 2 * s) for s in range(half)]
+    if back:
+        first, second = [(b, a) for a, b in first], [(b, a) for a, b in second]
+    return (
+        lax.ppermute(one, ("dp", "fsdp"), first),
+        lax.ppermute(two, ("dp", "fsdp"), second),
+    )
+
+
+def picked(choice, one, two):
+    return jnp.where(choice, one, two), jnp.where(choice, two, one)
+
+
+def to_workers(block):
+    here = lax.axis_index(("dp", "fsdp"))
     half = lax.axis_size("dp") * lax.axis_size("fsdp") // 2
     size = block.shape[2] // 2
-    low, high = block[:, :, :size], block[:, :, size:]
-    even = lax.ppermute(low, ("dp", "fsdp"), [(first + s, 2 * s) for s in range(half)])
-    odd = lax.ppermute(high, ("dp", "fsdp"), [(first + s, 2 * s + 1) for s in range(half)])
-    return even + odd
-
-
-def to_owners(piece, first):
-    half = lax.axis_size("dp") * lax.axis_size("fsdp") // 2
-    even = lax.ppermute(piece, ("dp", "fsdp"), [(2 * s, first + s) for s in range(half)])
-    odd = lax.ppermute(piece, ("dp", "fsdp"), [(2 * s + 1, first + s) for s in range(half)])
-    return even, odd
+    sent = picked(here < half, block[:, :, :size], block[:, :, size:])
+    return moved(*sent, False)
+
+
+def to_owners(front, gate):
+    here = lax.axis_index(("dp", "fsdp"))
+    return moved(*picked(here % 2 == 0, front, gate), True)
 
 
 def shifted(value, axis, steps):
@@ -410,7 +498,9 @@
         ],
         axis=0,
     )
-    packed = in_order(lax.all_gather(packed, "fsdp", axis=1, tiled=True), parts)
+    packed = lax.all_gather(packed, "fsdp", axis=1, tiled=True)
+    packed, out_block = then(packed, out_weight)
+    packed = in_order(packed, parts)
     sizes = [1, taps, 1, copies, states, 1, copies * rank, copies * (rank + 2 * states)]
     rows, at = [], 0
     for size in sizes:
@@ -423,25 +513,31 @@
     select_full = rows[7].reshape(copies, rank + 2 * states, width)
 
     small = jnp.concatenate([gain_part, modality.reshape(-1).astype(low)])
-    small = lax.all_gather(small[None], "dp", axis=0, tiled=True)
+    spare = -(-small.shape[0] // model)
+    spare = -(-spare // 16) * 16
+    small = jnp.pad(small, (0, spare * model - small.shape[0])).reshape(1, spare, model)
+    x_sent = jnp.concatenate([inputs.reshape(1, seq_count * length, model), small], axis=1)
+    columns = to_workers(in_weight)
+    out_parts = [out_block] + [exchanged(out_block, "fsdp", m) for m in range(1, parts)]
+    columns, out_parts, x_sent = then(columns, out_parts, x_sent)
+    x_all = lax.all_gather(x_sent, "dp", axis=0, tiled=True)
+    front_block, gate_block = picked(lax.axis_index(("dp", "fsdp")) % 2 == 0, *columns)
+    front_parts = [front_block] + [exchanged(front_block, "fsdp", m) for m in range(1, parts)]
+    front_parts, gate_block, g_sent = then(front_parts, gate_block, out_grad)
+    front_full = jnp.concatenate(front_parts, axis=2)
+    out_full = jnp.concatenate(out_parts, axis=1)
+    g_all = lax.all_gather(g_sent, "dp", axis=0, tiled=True).reshape(tokens, model)
+    small = x_all[:, seq_count * length :].reshape(groups, -1)
+    x_all = x_all[:, : seq_count * length].reshape(tokens, model)
     gain_full = small[:, : gain_part.shape[0]].reshape(model).astype(full)
-    kinds = small[:, gain_part.shape[0] :].reshape(count, length)
+    kinds = small[:, gain_part.shape[0] : gain_part.shape[0] + seq_count * length]
+    kinds = kinds.reshape(count, length)
     copy_ids = jnp.arange(copies, dtype=low)
 
     def masks_of(values):
         return (values.reshape(tokens)[:, None] == copy_ids[None, :]).astype(full)
 
     masks, masks_t = masks_of(kinds), masks_of(swap(kinds))
-
-    x_all = lax.all_gather(inputs, "dp", axis=0, tiled=True).reshape(tokens, model)
-    front_block = to_workers(in_weight, 0)
-    out_parts = [out_weight] + [exchanged(out_weight, "fsdp", m) for m in range(1, parts)]
-    out_parts, gate_from = then(out_parts, in_weight)
-    gate_block = to_workers(gate_from, groups * parts // 2)
-    x_all, g_sent = then(x_all, out_grad)
-    g_all = lax.all_gather(g_sent, "dp", axis=0, tiled=True).reshape(tokens, model)
-    front_full = gathered(front_block, "fsdp", 2)
-    out_full = jnp.concatenate(out_parts, axis=1)
 
     x_float = x_all.astype(full)
     inverse = lax.rsqrt(jnp.mean(x_float * x_float, axis=-1, keepdims=True) + epsilon)
@@ -452,6 +548,11 @@
 
     def by_sequence(value):
         return swap(value).reshape(tokens, value.shape[2])
+
+    def by_channel(value):
+        return jnp.transpose(value, (2, 1, 0)).reshape(value.shape[2], tokens)
+
+    masks_rows = jnp.transpose(masks).astype(low)
 
     u_pre = by_time(mode_dot(normed, front_full, masks).astype(low))
     rim = in_order(shifted(in_order(u_pre[length - (taps - 1) :], parts), "fsdp", 1), parts)
@@ -462,14 +563,14 @@
     u_act = jax.nn.silu(pre_conv)
     u_low = u_act.astype(low).reshape(tokens, width)
     proj = mode_dot_back(u_low, select_full, masks_t)
-    proj, g_then = then(proj, g_all)
-    kept_part, other = core_sent(proj.reshape(groups, tokens // groups, -1), full)
-    d_gated = mode_dot_back(g_then, out_full, masks)
-    other, d_gated = then(other, d_gated)
-    own, sent = chips_sent(kept_part, other, full)
-    column = chips_gathered(summed(own + chips_received(sent)))
-    column, gate_parts = then(column, gate_parts)
-    proj = core_gathered(column).reshape(tokens, -1)
+    proj, g_all = then(proj, g_all)
+    _, normed_then = then(proj, normed)
+    proj = lax.psum(proj, "dp")
+    gate_full = jnp.concatenate(gate_parts, axis=2)
+    z_low = mode_dot(normed_then, gate_full, masks).astype(low)
+    proj, z_low = then(proj, z_low)
+    z_gate = by_time(z_low).astype(full)
+    gate = jax.nn.silu(z_gate)
     dt_rank = proj[:, :rank].astype(low)
     maps = proj[:, rank:]
     top = lax.reduce_precision(maps, 8, 7)
@@ -500,15 +601,10 @@
         end_kernel, delta, states, False,
         [("rows", delta), ("rows", u_act)] + common, ["state", "sum"], ["spread"], 4,
     )
-    edge, normed_then, gate_parts = then(
-        jnp.concatenate([end, total[None]], axis=0), normed, gate_parts
-    )
+    edge, g_then = then(jnp.concatenate([end, total[None]], axis=0), g_all)
     edges = exchange_edge(edge)
-    gate_full = jnp.concatenate(gate_parts, axis=2)
-    z_low = mode_dot(normed_then, gate_full, masks).astype(low)
-    edges, z_low = then(edges, z_low)
-    z_gate = by_time(z_low).astype(full)
-    gate = jax.nn.silu(z_gate)
+    d_gated = mode_dot_back(g_then, out_full, masks)
+    edges, d_gated = then(edges, d_gated)
     d_gated = by_time(d_gated)
     d_y = d_gated * gate
     decays = [jnp.exp(rate[:, None, :] * other[states][None]) for other in edges]
@@ -526,24 +622,23 @@
     y_scan, aheads = then(y_scan, aheads)
     final = carried_in(decays, aheads, True)
     mixed_out = y_scan + skip_full * u_act
-    gated = by_sequence((mixed_out * gate).astype(low))
+    gated_low = (mixed_out * gate).astype(low)
+    gated = by_sequence(gated_low)
     sig_z = jax.nn.sigmoid(z_gate)
     d_z = d_gated * mixed_out * (sig_z * (1.0 + z_gate * (1.0 - sig_z)))
     d_gate = by_sequence(d_z.astype(low))
 
-    def lowered(grad):
-        return [grad[:, 0]] + [grad[:, m].astype(low) for m in range(1, parts)]
-
     def fsdp_received(pieces):
-        return pieces[:1] + [exchanged(pieces[m], "fsdp", m) for m in range(1, parts)]
-
-    gate_grad = lowered(mode_outer(d_gate, normed, masks).reshape(copies, parts, block, model))
+        return [pieces[0]] + [exchanged(pieces[m], "fsdp", m) for m in range(1, parts)]
+
+    gate_grad = outer_pieces(by_channel(d_z.astype(low)), normed, masks_rows, parts)
     gate_grad, gated = then(gate_grad, gated)
     out_sent = mode_dot(gated, out_full, masks).astype(low).reshape(count, length, model)
     out_sent, gated = then(out_sent, gated)
     out_rows = lax.psum_scatter(out_sent, "dp", scatter_dimension=0, tiled=True)
 
-    outer_grad = lowered(mode_outer(gated, g_all, masks).reshape(copies, parts, block, model))
+    _, gated_low = then(out_sent, gated_low)
+    outer_grad = outer_pieces(by_channel(gated_low), g_all, masks_rows, parts)
     d_u_scan, d_delta, d_maps, rate_part = scan_call(
         backward_kernel, delta, states, True,
         [("rows", delta), ("rows", u_act), ("rows", d_y)] + common
@@ -552,30 +647,27 @@
         after=(out_sent, gate_grad[-1], outer_grad[-1]),
     )
     gate_received, outer_received = fsdp_received(gate_grad), fsdp_received(outer_grad)
-    d_u_scan, d_delta, d_maps, rate_part, gate_received, outer_received = then(
-        d_u_scan, d_delta, d_maps, rate_part, gate_received, outer_received
+    d_u_scan, d_delta, d_maps, rate_part, gate_received = then(
+        d_u_scan, d_delta, d_maps, rate_part, gate_received
     )
     gate_piece = jnp.swapaxes(summed(gate_received).astype(low), 1, 2)
-    out_weight_grad = summed(outer_received)
     rate_grad = rate * jnp.sum(rate_part, axis=1)
     d_raw = (d_delta * jax.nn.sigmoid(raw)).astype(low).reshape(tokens, width)
     d_rank = mode_dot_back(d_raw, step_full, masks_t)
     d_proj = jnp.concatenate([d_rank, d_maps.reshape(tokens, 2 * states)], axis=1)
-    d_proj, d_gate = then(d_proj, d_gate)
-    kept_part, other = core_sent(d_proj.reshape(groups, tokens // groups, -1), full)
+    d_proj, d_gate, out_rows = then(d_proj, d_gate, out_rows)
+    d_proj = lax.psum(d_proj, "dp")
     d_normed_gate = mode_dot_back(d_gate, gate_full, masks)
     skip_grad = jnp.sum(d_y * u_act, axis=(0, 1))
     step_grad = mode_outer(dt_rank, d_raw, masks_t)
     sbias_grad = lax.dot_general(
         masks_t.astype(low), d_raw, (((0,), (0,)), ((), ())), preferred_element_type=full
     )
-    other, d_normed_gate = then(other, d_normed_gate)
-    own, sent = chips_sent(kept_part, other, full)
-    own = summed(own + chips_received(sent)).astype(low)
-    d_proj = core_gathered(chips_gathered(own)).reshape(tokens, -1)
-    d_proj, gate_piece, skip_grad, step_grad, sbias_grad, out_rows = then(
-        d_proj, gate_piece, skip_grad, step_grad, sbias_grad, out_rows
-    )
+    d_proj, d_normed_gate, skip_grad, step_grad, sbias_grad, outer_received = then(
+        d_proj, d_normed_gate, skip_grad, step_grad, sbias_grad, outer_received
+    )
+    out_weight_grad = summed(outer_received)
+    d_proj = lax.reduce_precision(d_proj, 8, 7).astype(low)
     output = (inputs.astype(full) + out_rows.astype(full)).astype(low)
     gate_even, gate_odd = to_owners(gate_piece, groups * parts // 2)
     d_u = (
@@ -588,20 +680,26 @@
     rim_back = shifted(in_order(d_conv[: taps - 1].astype(low), parts), "fsdp", -1)
     d_ahead = jnp.concatenate([d_conv, in_order(rim_back, parts).astype(full)], axis=0)
     d_u_pre = convolve(d_ahead, conv_full[::-1], 0.0, length)
-    d_front = by_sequence(d_u_pre.astype(low))
-    d_normed = d_normed_gate + mode_dot_back(d_front, front_full, masks)
-    d_sent = d_normed.astype(low).reshape(groups, seq_count, length, model)
-    d_sent, d_front, gate_even, gate_odd = then(d_sent, d_front, gate_even, gate_odd)
-    kept_part, other = core_sent(d_sent, low)
-    gain_part = jnp.sum(d_normed * x_float * inverse, axis=0)
-    gain_part, d_front = then(gain_part, d_front)
+    d_u_low = d_u_pre.astype(low)
+    d_front = by_sequence(d_u_low)
+    d_front = d_front[None] * jnp.transpose(masks)[:, :, None].astype(low)
+    d_sent = product_back(d_front, front_full, d_normed_gate)
+    d_rows = lax.psum_scatter(
+        d_sent.reshape(count, length, model), "dp", scatter_dimension=0, tiled=True
+    ).astype(full)
+    gain_part = jnp.sum(d_sent.astype(full) * x_float * inverse, axis=0)
+    gain_part, d_u_low = then(gain_part, d_u_low)
+    front_pieces = outer_pieces(by_channel(d_u_low), normed, masks_rows, parts)
+    front_received = fsdp_received(front_pieces)
+    _, gain_part = then(front_pieces, gain_part)
     gain_kept, gain_other = core_sent(gain_part.reshape(groups, -1), full)
     gain_own, gain_sent = chips_sent(gain_kept, gain_other, full)
     gain_part = summed(gain_own + chips_received(gain_sent))
-    front_pieces = lowered(mode_outer(d_front, normed, masks).reshape(copies, parts, block, model))
-    front_pieces, gain_part, d_conv, u_low = then(front_pieces, gain_part, d_conv, u_low)
-
-    gain_rows = jnp.pad(gain_part.reshape(parts, -1), ((0, 0), (0, block - gain.shape[0])))
+    gain_row = jnp.pad(gain_part.reshape(parts, -1), ((0, 0), (0, block - gain.shape[0])))
+    front_received, gain_row, d_conv, u_low = then(front_received, gain_row, d_conv, u_low)
+    front_piece = jnp.swapaxes(summed(front_received).astype(low), 1, 2)
+    returned = to_owners(front_piece, gate_piece)
+
     select_grad = mode_outer(d_proj, u_low, masks_t)
     cshift_grad = jnp.sum(d_conv, axis=(0, 1))
     conv_grad = jnp.stack(
@@ -616,23 +714,14 @@
             skip_grad[None],
             step_grad.reshape(copies * rank, width),
             select_grad.reshape(-1, width),
+            in_order(gain_row.reshape(1, width), parts),
         ],
         axis=0,
     )
-    grads = jnp.concatenate([in_order(grads, parts), gain_rows.reshape(1, width)], axis=0)
-    other, front_pieces, grads = then(other, front_pieces, grads)
-    own, sent = chips_sent(kept_part, other, low)
-    rows_received = chips_received(sent)
-    front_received = fsdp_received(front_pieces)
-    sent, grads = then(sent, grads)
-    grads = lax.psum_scatter(grads, "fsdp", scatter_dimension=1, tiled=True)
+    grads = summed(fsdp_received([grads[:, m * block : (m + 1) * block] for m in range(parts)]))
     gain_grad = grads[-1, : gain.shape[0]]
-
-    front_even, front_odd = to_owners(
-        jnp.swapaxes(summed(front_received).astype(low), 1, 2), 0
-    )
-    in_weight_grad = jnp.concatenate([gate_even + front_even, gate_odd + front_odd], axis=2).astype(full)
-    d_rows = summed(own + rows_received)
+    halves = picked(lax.axis_index(("dp", "fsdp")) < groups * parts // 2, *returned)
+    in_weight_grad = jnp.concatenate(halves, axis=2).astype(full)
     own = inputs.astype(full)
     own_inverse = lax.rsqrt(jnp.mean(own * own, axis=-1, keepdims=True) + epsilon)
     d_scaled = d_rows * gain_full

time: 1300 us -> 1090 us (0.84)
  blocking collectives: 149 us -> 46.5 us
  matrix products: 201 us -> 124 us
  Pallas kernels: 156 us -> 229 us
  waiting for transfers between devices: 413 us -> 374 us
  local copies, waits for them, and re-layouts: 139 us -> 108 us
  starting transfers between devices: 83.9 us -> 55.3 us
  other arithmetic: 138 us -> 122 us
    all_gather x1, waiting for transfers between devices: 91.1 us -> 0.01 us  [shards(): x_all = lax.all_gather(x_sent, 'dp', axis=0, tiled=True)]
    pallas_call x0 -> x4, Pallas kernels: none -> 83.4 us  [the longest x3 57.6 us: outer_pieces(): pl.pallas_call(outer_kernel, grid=(columns // tile,), in_specs=[pl.BlockS...]
    ppermute x8 -> x4, waiting for transfers between devices: 86.6 us -> 15.2 us  [the longest x2 15.2 us: moved(): lax.ppermute(two, ('dp', 'fsdp'), second)]
    unnamed x1 -> x0, blocking collectives: 68.9 us -> none
    ppermute x48 -> x31, waiting for transfers between devices: 235 us -> 301 us  [exchanged(): lax.ppermute(value, axis, [(source, source ^ mask) for source in range(co...]
    dot_general x5 -> x2, matrix products: 61.4 us -> 4.24 us  [mode_outer(): lax.dot_general(masked(left, masks), right, (((0,), (0,)), ((), ())), pre...]
    all_gather x1, blocking collectives: 80.5 us -> 46.5 us  [shards(): packed = lax.all_gather(packed, 'fsdp', axis=1, tiled=True)]
    psum x0 -> x2, waiting for transfers between devices: none -> 27.7 us  [the longest x1 14.9 us: shards(): proj = lax.psum(proj, 'dp')]
  transfers between devices with their start and end apart: 62 -> 43, of which waited for: 23 -> 19; matrix products, arithmetic and copies ran while one was open for 27% -> 23% of each run, Pallas kernels for 9% -> 14%
where the time goes in v2:
time: 1090 us; the launch traced here: 1080 us
  waiting for transfers between devices  374 us (34%)
  Pallas kernels  229 us (21%)
  matrix products  124 us (11%)
  other arithmetic  122 us (11%)
  local copies, waits for them, and re-layouts  108 us (10%)
  starting transfers between devices  55.3 us (5%)
  blocking collectives  46.5 us (4%)
  between operations  15.9 us (1%)
    ppermute x31, waiting for transfers between devices, exchanged(): lax.ppermute(value, axis, [(source, source ^ mask) for source in range(co...  301 us
    pallas_call x4, Pallas kernels, scan_call(): pl.pallas_call(kernel, grid=(count // SUB, steps), in_specs=[specs[name][...  146 us
    dot_general x5, matrix products, mode_dot(): lax.dot_general(masked(left, masks), weight, (((1, 2), (0, 1)), ((), ()))...  71.8 us
    pallas_call x3, Pallas kernels, outer_pieces(): pl.pallas_call(outer_kernel, grid=(columns // tile,), in_specs=[pl.BlockS...  57.6 us
    dot_general x4, matrix products, mode_dot_back(): lax.dot_general(masked(left, masks), weight, (((1, 2), (0, 2)), ((), ()))...  47.9 us
    all_gather x1, blocking collectives, shards(): packed = lax.all_gather(packed, 'fsdp', axis=1, tiled=True)  46.5 us
    ppermute x31, starting transfers between devices, exchanged(): lax.ppermute(value, axis, [(source, source ^ mask) for source in range(co...  41.3 us
    unnamed x189, local copies, waits for them, and re-layouts  41.1 us
  transfers between devices with their start and end apart: 43, of which 19 were waited for; matrix products, arithmetic and copies ran while one was open for 23% of the time, Pallas kernels for 14%

profile of v2, /device:TPU:10, one launch (start us, length us, event | category | flops | bytes accessed | tf_op | source)
XLA Modules:
  0.0 1075.7 jit_solution(15146968295407808289)
XLA Ops:
  21.0 46.5 %all_gather.9 = bf16[890,512]{1,0:T(8,128)(2,1)S(1)} all-gather(bf16[890,128]{1,0:T(8,128)(2,1)S(1)} %concatenate.91), channel_id=1, replica_groups=mesh['dp'=8,'fsdp'=4] {'fsdp'}, dimensions={1}, use_global_device_ids=true | all-gather | bytes 1139200 | tf_op jit(solution)/shard_map/all_gather | solution.py:501
  72.8 15.2 %collective-permute-done.1 = bf16[3,2048,128]{1,2,0:T(8,128)(2,1)} collective-permute-done((bf16[3,2048,128]{1,2,0:T(8,128)(2,1)}, bf16[3,2048,128]{1,2,0:T(8,128)(2,1)}, u32[]{:S(2)}, u32[]{:S(2)}) %collective-permute-start.1) | collective-permute-done | bytes 1572896 | tf_op jit(solution)/shard_map/ppermute | solution.py:413
  88.0 22.3 %collective-permute-done.2 = bf16[3,128,2048]{2,1,0:T(8,128)(2,1)} collective-permute-done((bf16[3,128,2048]{2,1,0:T(8,128)(2,1)}, bf16[3,128,2048]{2,1,0:T(8,128)(2,1)}, u32[]{:S(2)}, u32[]{:S(2)}) %collective-permute-start.2) | collective-permute-done | bytes 1572896 | tf_op jit(solution)/shard_map/ppermute | solution.py:341
  110.3 33.7 %collective-permute-done.4 = bf16[3,128,2048]{2,1,0:T(8,128)(2,1)} collective-permute-done((bf16[3,128,2048]{2,1,0:T(8,128)(2,1)}, bf16[3,128,2048]{2,1,0:T(8,128)(2,1)}, u32[]{:S(2)}, u32[]{:S(2)}) %collective-permute-start.4) | collective-permute-done | bytes 1572896 | tf_op jit(solution)/shard_map/ppermute | solution.py:341
  151.9 31.5 %collective-permute-done.5 = bf16[3,2048,128]{1,2,0:T(8,128)(2,1)S(1)} collective-permute-done((bf16[3,2048,128]{1,2,0:T(8,128)(2,1)S(1)}, bf16[3,2048,128]{1,2,0:T(8,128)(2,1)S(1)}, u32[]{:S(2)}, u32[]{:S(2)}) %collective-permute-start.5) | collective-permute-done | bytes 1572896 | tf_op jit(solution)/shard_map/ppermute | solution.py:341
  183.4 35.6 %collective-permute-done.6 = bf16[3,2048,128]{1,2,0:T(8,128)(2,1)S(1)} collective-permute-done((bf16[3,2048,128]{1,2,0:T(8,128)(2,1)S(1)}, bf16[3,2048,128]{1,2,0:T(8,128)(2,1)S(1)}, u32[]{:S(2)}, u32[]{:S(2)}) %collective-permute-start.6) | collective-permute-done | bytes 1572896 | tf_op jit(solution)/shard_map/ppermute | solution.py:341
  248.6 10.4 fusion.8.right_ref
  259.0 21.1 %fusion.63 = bf16[2304,512]{1,0:T(8,128)(2,1)} fusion(bf16[3,2048,512]{1,2,0:T(8,128)(2,1)} %constant_dynamic-update-slice_fusion, bf16[2304,3]{0,1:T(4,128)(2,1)S(1)} %convert_convert_fusion.2, bf16[2304,2048]{1,0:T(8,128)(2,1)} %fusion.8.right_ref), kind=kOutput, calls=%fused_computation.83 | convolution fusion | flops 14510850048 | bytes 18101760 | tf_op jit(solution)/shard_map/dot_general | solution.py:247
  304.0 27.3 %all-gather.5.cloned.1.call-done = bf16[8,288,2048]{2,1,0:T(8,128)(2,1)} async-done(((bf16[1,288,2048]{2,1,0:T(8,128)(2,1)}), bf16[8,288,2048]{2,1,0:T(8,128)(2,1)}) %all-gather.5.cloned.1.call-update) | async-done | bytes 9437200 | tf_op jit(solution)/shard_map/all_gather | solution.py:529
  336.0 24.0 %collective-permute-done.10 = bf16[3,2048,128]{1,2,0:T(8,128)(2,1)} collective-permute-done((bf16[3,2048,128]{1,2,0:T(8,128)(2,1)}, bf16[3,2048,128]{1,2,0:T(8,128)(2,1)}, u32[]{:S(2)}, u32[]{:S(2)}) %collective-permute-start.10) | collective-permute-done | bytes 1572896 | tf_op jit(solution)/shard_map/ppermute | solution.py:341
  365.6 20.7 %fusion.60 = bf16[2304,512]{1,0:T(8,128)(2,1)} fusion(bf16[3,2048,512]{1,2,0:T(8,128)(2,1)} %constant_dynamic-update-slice_fusion.4, bf16[2304,2048]{1,0:T(8,128)(2,1)} %fusion.8.right_ref, bf16[2304,3]{0,1:T(4,128)(2,1)S(1)} %convert_convert_fusion.2), kind=kOutput, calls=%fused_computation.82 | convolution fusion | flops 14510850048 | bytes 18101760 | tf_op jit(solution)/shard_map/dot_general | solution.py:247
  386.3 14.9 %all-reduce.6.cloned.1.call-done = f32[2304,160]{1,0:T(8,128)} async-done(((f32[2304,160]{1,0:T(8,128)}), f32[2304,160]{1,0:T(8,128)}) %all-reduce.6.cloned.1.call-update) | async-done | bytes 1474576 | tf_op jit(solution)/shard_map/psum | solution.py:568
  413.1 19.8 %shard_map.220 = (f32[16,8,512]{2,1,0:T(8,128)S(1)}, f32[8,512]{1,0:T(8,128)S(1)}) custom-call(f32[288,8,512]{2,1,0:T(8,128)S(1)} %get-tuple-element.380.d_ref, f32[288,8,512]{2,1,0:T(8,128)S(1)} %bitcast.387, bf16[1,2304,96]{2,1,0:T(8,128)(2,1)S(1)} %pad_maximum_fusion.8.parts_ref, bf16[96,4096]{1,0:T(8,128)(2,1)S(1)} %compare_convert_fusion.ones_ref, ...), custom_call_target="tpu_custom_call" | custom-call | flops 22649241600 | bytes 33030144 | tf_op jit(solution)/shard_map/pallas_call | solution.py:225
  436.4 21.0 %fusion.29 = f32[2304,512]{1,0:T(8,128)} fusion(bf16[3,512,2048]{2,1,0:T(8,128)(2,1)} %constant_dynamic-update-slice_fusion.8, bf16[2304,2048]{1,0:T(8,128)(2,1)} %bitcast.416, bf16[2304,3]{0,1:T(4,128)(2,1)S(1)} %convert_convert_fusion.2), kind=kOutput, calls=%fused_computation.34 | convolution fusion | flops 14509670400 | bytes 20461056 | tf_op jit(solution)/shard_map/dot_general | solution.py:253
  468.1 18.6 %shard_map.221.refs_0_ = f32[16,8,512]{2,1,0:T(8,128)S(1)} custom-call(f32[288,8,512]{2,1,0:T(8,128)S(1)} %bitcast.398, f32[288,8,512]{2,1,0:T(8,128)S(1)} %get-tuple-element.258.y_ref, bf16[1,2304,96]{2,1,0:T(8,128)(2,1)S(1)} %pad_maximum_fusion.8.parts_ref, bf16[96,4096]{1,0:T(8,128)(2,1)S(1)} %compare_convert_fusion.ones_ref, ...), custom_call_target="tpu_custom_call" | custom-call | flops 22649241600 | bytes 28311552 | tf_op jit(solution)/shard_map/pallas_call | solution.py:225
  490.8 28.6 %shard_map.222 = (f32[288,8,512]{2,1,0:T(8,128)S(1)}, f32[18,16,8,512]{3,2,1,0:T(8,128)S(1)}) custom-call(f32[288,8,512]{2,1,0:T(8,128)} %copy-done.3, f32[288,8,512]{2,1,0:T(8,128)} %get-tuple-element.262.u_ref, bf16[1,2304,96]{2,1,0:T(8,128)(2,1)S(1)} %pad_maximum_fusion.8.parts_ref, bf16[96,4096]{1,0:T(8,128)(2,1)S(1)} %compare_convert_fusion.ones_ref, ...), custom_call_target="tpu_custom_call" | custom-call | flops 33973862400 | bytes 37748736 | tf_op jit(solution)/shard_map/pallas_call | solution.py:225
  520.6 9.5 multiply_convert_fusion
  540.5 19.0 %shard_map.223 = (f32[3,128,2048]{2,1,0:T(8,128)}, bf16[3,128,2048]{2,1,0:T(8,128)(2,1)}, bf16[3,128,2048]{2,1,0:T(8,128)(2,1)}, bf16[3,128,2048]{2,1,0:T(8,128)(2,1)}) custom-call(bf16[512,2304]{1,0:T(8,128)(2,1)} %copy.103.left_ref, bf16[2304,2048]{1,0:T(8,128)(2,1)} %fusion.8.right_ref, bf16[3,2304]{1,0:T(4,128)(2,1)} %convert_convert_fusion.1.masks_ref), custom_call_target="tpu_custom_call" | custom-call | flops 1000 | bytes 1000 | tf_op jit(solution)/shard_map/pallas_call | solution.py:282
  559.5 19.2 %bitcast_convert_fusion = bf16[2304,2048]{1,0:T(8,128)(2,1)} fusion(bf16[3,512,2048]{2,1,0:T(8,128)(2,1)} %constant_dynamic-update-slice_fusion.8, bf16[2304,3]{0,1:T(4,128)(2,1)S(1)} %convert_convert_fusion.2, bf16[2304,512]{1,0:T(8,128)(2,1)S(1)} %bitcast.426), kind=kOutput, calls=%fused_computation.6 | convolution fusion | flops 14503772160 | bytes 18101760 | tf_op jit(solution)/shard_map/dot_general | solution.py:247
  588.0 19.2 %shard_map.224 = (f32[3,128,2048]{2,1,0:T(8,128)}, bf16[3,128,2048]{2,1,0:T(8,128)(2,1)}, bf16[3,128,2048]{2,1,0:T(8,128)(2,1)}, bf16[3,128,2048]{2,1,0:T(8,128)(2,1)}) custom-call(bf16[512,2304]{1,0:T(8,128)(2,1)} %copy.106.left_ref, bf16[2304,2048]{1,0:T(8,128)(2,1)} %bitcast.417, bf16[3,2304]{1,0:T(4,128)(2,1)} %convert_convert_fusion.1.masks_ref), custom_call_target="tpu_custom_call" | custom-call | flops 1000 | bytes 1000 | tf_op jit(solution)/shard_map/pallas_call | solution.py:282
  616.2 78.7 %shard_map.225 = (f32[288,8,512]{2,1,0:T(8,128)S(1)}, f32[288,8,512]{2,1,0:T(8,128)}, f32[288,8,32]{2,1,0:T(8,128)S(1)}, f32[16,8,512]{2,1,0:T(8,128)S(1)}) custom-call(f32[288,8,512]{2,1,0:T(8,128)} %copy-done.3, f32[288,8,512]{2,1,0:T(8,128)} %get-tuple-element.262.u_ref, f32[288,8,512]{2,1,0:T(8,128)} %copy-done, ...), custom_call_target="tpu_custom_call" | custom-call | flops 90596966400 | bytes 56623104 | tf_op jit(solution)/shard_map/pallas_call | solution.py:225
  715.5 20.9 %convolution_bitcast_fusion.base_ref = f32[2304,2048]{1,0:T(8,128)} fusion(bf16[3,2048,512]{1,2,0:T(8,128)(2,1)} %constant_dynamic-update-slice_fusion.4, bf16[2304,512]{1,0:T(8,128)(2,1)S(1)} %bitcast.425, bf16[2304,3]{0,1:T(4,128)(2,1)S(1)} %copy-done.51), kind=kOutput, calls=%fused_computation.22 | convolution fusion | flops 14499053568 | bytes 27538944 | tf_op jit(solution)/shard_map/dot_general | solution.py:253
  736.5 26.6 %collective-permute-done.22 = bf16[3,128,2048]{2,1,0:T(8,128)(2,1)} collective-permute-done((bf16[3,128,2048]{2,1,0:T(8,128)(2,1)}, bf16[3,128,2048]{2,1,0:T(8,128)(2,1)}, u32[]{:S(2)}, u32[]{:S(2)}) %collective-permute-start.22) | collective-permute-done | bytes 1572896 | tf_op jit(solution)/shard_map/ppermute | solution.py:341
  763.1 12.8 %all-reduce.8.cloned.1.call-done = f32[2304,160]{0,1:T(8,128)} async-done(((f32[2304,160]{0,1:T(8,128)}), f32[2304,160]{0,1:T(8,128)}) %all-reduce.8.cloned.1.call-update) | async-done | bytes 1474576 | tf_op jit(solution)/shard_map/psum | solution.py:659
  790.4 9.1 copy.112.weight_ref
  811.7 25.8 %shard_map.226 = bf16[2304,2048]{1,0:T(8,128)(2,1)} custom-call(bf16[3,2304,512]{2,1,0:T(8,128)(2,1)} %broadcast_multiply_fusion.left_ref, bf16[3,2048,512]{2,1,0:T(8,128)(2,1)} %copy.112.weight_ref, f32[2304,2048]{1,0:T(8,128)} %convolution_bitcast_fusion.base_ref), custom_call_target="tpu_custom_call" | custom-call | flops 14495514624 | bytes 28311552 | tf_op jit(solution)/shard_map/pallas_call | solution.py:320
  838.2 10.1 fusion.10
  854.8 19.4 %shard_map.227 = (f32[3,128,2048]{2,1,0:T(8,128)}, bf16[3,128,2048]{2,1,0:T(8,128)(2,1)}, bf16[3,128,2048]{2,1,0:T(8,128)(2,1)}, bf16[3,128,2048]{2,1,0:T(8,128)(2,1)}) custom-call(bf16[512,2304]{1,0:T(8,128)(2,1)} %copy.114.left_ref, bf16[2304,2048]{1,0:T(8,128)(2,1)} %fusion.8.right_ref, bf16[3,2304]{1,0:T(4,128)(2,1)} %convert_convert_fusion.1.masks_ref), custom_call_target="tpu_custom_call" | custom-call | flops 1000 | bytes 1000 | tf_op jit(solution)/shard_map/pallas_call | solution.py:282
  887.8 24.1 %collective-permute-done.25 = bf16[3,128,2048]{2,1,0:T(8,128)(2,1)} collective-permute-done((bf16[3,128,2048]{2,1,0:T(8,128)(2,1)}, bf16[3,128,2048]{2,1,0:T(8,128)(2,1)}, u32[]{:S(2)}, u32[]{:S(2)}) %collective-permute-start.25) | collective-permute-done | bytes 1572896 | tf_op jit(solution)/shard_map/ppermute | solution.py:341
  911.9 30.5 %collective-permute-done.26 = bf16[3,128,2048]{2,1,0:T(8,128)(2,1)} collective-permute-done((bf16[3,128,2048]{2,1,0:T(8,128)(2,1)}, bf16[3,128,2048]{2,1,0:T(8,128)(2,1)}, u32[]{:S(2)}, u32[]{:S(2)}) %collective-permute-start.26) | collective-permute-done | bytes 1572896 | tf_op jit(solution)/shard_map/ppermute | solution.py:341
  943.2 9.0 select_bitcast_fusion.1
  977.1 60.8 %collective-permute-done.34 = f32[890,128]{1,0:T(8,128)S(1)} collective-permute-done((f32[890,128]{1,0:T(8,128)S(1)}, f32[890,128]{1,0:T(8,128)S(1)}, u32[]{:S(2)}, u32[]{:S(2)}) %collective-permute-start.34) | collective-permute-done | bytes 455712 | tf_op jit(solution)/shard_map/ppermute | solution.py:341
  (426 shorter events, 274.0 us)
Async XLA Ops:
  7.2 234.0 %all-gather.3.cloned.1.call-start = ((), (), s32[]{:S(2)}) async-start(), calls=%async_computation.2 | async-start | bytes 11206656 | tf_op jit(solution)/shard_map/all_gather | solution.py:523
  15.0 57.8 %collective-permute-start = (bf16[3,2048,128]{1,2,0:T(8,128)(2,1)}, bf16[3,2048,128]{1,2,0:T(8,128)(2,1)}, u32[]{:S(2)}, u32[]{:S(2)}) collective-permute-start(bf16[3,2048,128]{1,2,0:T(8,128)(2,1)} %get-tuple-element.271), channel_id=1, source_target_pairs={{0,0},{1,2},{2,4},{3,6},{4,8},{5,10},{6,12},{7,14},{8,16},{9,18},{... | collective-permute-start | bytes 4718600 | tf_op jit(solution)/shard_map/ppermute | solution.py:412
  19.5 68.5 %collective-permute-start.1 = (bf16[3,2048,128]{1,2,0:T(8,128)(2,1)}, bf16[3,2048,128]{1,2,0:T(8,128)(2,1)}, u32[]{:S(2)}, u32[]{:S(2)}) collective-permute-start(bf16[3,2048,128]{1,2,0:T(8,128)(2,1)} %get-tuple-element.270), channel_id=1, source_target_pairs={{0,1},{1,3},{2,5},{3,7},{4,9},{5,11},{6,13},{7,15},{8,17},{9,19},{... | collective-permute-start | bytes 4718600 | tf_op jit(solution)/shard_map/ppermute | solution.py:413
  67.5 42.8 %collective-permute-start.2 = (bf16[3,128,2048]{2,1,0:T(8,128)(2,1)}, bf16[3,128,2048]{2,1,0:T(8,128)(2,1)}, u32[]{:S(2)}, u32[]{:S(2)}) collective-permute-start(bf16[3,128,2048]{2,1,0:T(8,128)(2,1)} %param.24), channel_id=1, source_target_pairs={{0,1},{1,0},{2,3},{3,2},{4,5},{5,4},{6,7},{7,6},{8,9},{9,8},{10,11... | collective-permute-start | bytes 4718600 | tf_op jit(solution)/shard_map/ppermute | solution.py:341
  67.5 42.8 %collective-permute-start.3 = (bf16[3,128,2048]{2,1,0:T(8,128)(2,1)}, bf16[3,128,2048]{2,1,0:T(8,128)(2,1)}, u32[]{:S(2)}, u32[]{:S(2)}) collective-permute-start(bf16[3,128,2048]{2,1,0:T(8,128)(2,1)} %param.24), channel_id=1, source_target_pairs={{0,2},{1,3},{2,0},{3,1},{4,6},{5,7},{6,4},{7,5},{8,10},{9,11},{10,... | collective-permute-start | bytes 4718600 | tf_op jit(solution)/shard_map/ppermute | solution.py:341
  68.6 75.4 %collective-permute-start.4 = (bf16[3,128,2048]{2,1,0:T(8,128)(2,1)}, bf16[3,128,2048]{2,1,0:T(8,128)(2,1)}, u32[]{:S(2)}, u32[]{:S(2)}) collective-permute-start(bf16[3,128,2048]{2,1,0:T(8,128)(2,1)} %param.24), channel_id=1, source_target_pairs={{0,3},{1,2},{2,1},{3,0},{4,7},{5,6},{6,5},{7,4},{8,11},{9,10},{10,... | collective-permute-start | bytes 4718600 | tf_op jit(solution)/shard_map/ppermute | solution.py:341
  144.0 187.3 %all-gather.5.cloned.1.call-start = ((), (), s32[]{:S(2)}) async-start(), calls=%async_computation.3 | async-start | bytes 10616832 | tf_op jit(solution)/shard_map/all_gather | solution.py:529
  147.3 36.1 %collective-permute-start.5 = (bf16[3,2048,128]{1,2,0:T(8,128)(2,1)S(1)}, bf16[3,2048,128]{1,2,0:T(8,128)(2,1)S(1)}, u32[]{:S(2)}, u32[]{:S(2)}) collective-permute-start(bf16[3,2048,128]{1,2,0:T(8,128)(2,1)S(1)} %get-tuple-element.108), channel_id=1, source_target_pairs={{0,1},{1,0},{2,3},{3,2},{4,5},{5,4},{6,7},{7,6},{8,9},{9,8},{10,11... | collective-permute-start | bytes 4718600 | tf_op jit(solution)/shard_map/ppermute | solution.py:341
  149.7 69.4 %collective-permute-start.6 = (bf16[3,2048,128]{1,2,0:T(8,128)(2,1)S(1)}, bf16[3,2048,128]{1,2,0:T(8,128)(2,1)S(1)}, u32[]{:S(2)}, u32[]{:S(2)}) collective-permute-start(bf16[3,2048,128]{1,2,0:T(8,128)(2,1)S(1)} %get-tuple-element.108), channel_id=1, source_target_pairs={{0,2},{1,3},{2,0},{3,1},{4,6},{5,7},{6,4},{7,5},{8,10},{9,11},{10,... | collective-permute-start | bytes 4718600 | tf_op jit(solution)/shard_map/ppermute | solution.py:341
  151.3 67.7 %collective-permute-start.7 = (bf16[3,2048,128]{1,2,0:T(8,128)(2,1)S(1)}, bf16[3,2048,128]{1,2,0:T(8,128)(2,1)S(1)}, u32[]{:S(2)}, u32[]{:S(2)}) collective-permute-start(bf16[3,2048,128]{1,2,0:T(8,128)(2,1)S(1)} %get-tuple-element.108), channel_id=1, source_target_pairs={{0,3},{1,2},{2,1},{3,0},{4,7},{5,6},{6,5},{7,4},{8,11},{9,10},{10,... | collective-permute-start | bytes 4718600 | tf_op jit(solution)/shard_map/ppermute | solution.py:341
  221.4 179.8 %all-reduce.6.cloned.1.call-start = ((), (), s32[]{:S(2)}) async-start(), calls=%async_computation.4 | async-start | bytes 4718592 | tf_op jit(solution)/shard_map/psum | solution.py:568
  288.9 44.4 %collective-permute-start.9 = (bf16[3,2048,128]{1,2,0:T(8,128)(2,1)}, bf16[3,2048,128]{1,2,0:T(8,128)(2,1)}, u32[]{:S(2)}, u32[]{:S(2)}) collective-permute-start(bf16[3,2048,128]{1,2,0:T(8,128)(2,1)} %get-tuple-element.117), channel_id=1, source_target_pairs={{0,1},{1,0},{2,3},{3,2},{4,5},{5,4},{6,7},{7,6},{8,9},{9,8},{10,11... | collective-permute-start | bytes 4718600 | tf_op jit(solution)/shard_map/ppermute | solution.py:341
  289.0 71.0 %collective-permute-start.10 = (bf16[3,2048,128]{1,2,0:T(8,128)(2,1)}, bf16[3,2048,128]{1,2,0:T(8,128)(2,1)}, u32[]{:S(2)}, u32[]{:S(2)}) collective-permute-start(bf16[3,2048,128]{1,2,0:T(8,128)(2,1)} %get-tuple-element.117), channel_id=1, source_target_pairs={{0,2},{1,3},{2,0},{3,1},{4,6},{5,7},{6,4},{7,5},{8,10},{9,11},{10,... | collective-permute-start | bytes 4718600 | tf_op jit(solution)/shard_map/ppermute | solution.py:341
  292.0 70.8 %collective-permute-start.11 = (bf16[3,2048,128]{1,2,0:T(8,128)(2,1)}, bf16[3,2048,128]{1,2,0:T(8,128)(2,1)}, u32[]{:S(2)}, u32[]{:S(2)}) collective-permute-start(bf16[3,2048,128]{1,2,0:T(8,128)(2,1)} %get-tuple-element.117), channel_id=1, source_target_pairs={{0,3},{1,2},{2,1},{3,0},{4,7},{5,6},{6,5},{7,4},{8,11},{9,10},{10,... | collective-permute-start | bytes 4718600 | tf_op jit(solution)/shard_map/ppermute | solution.py:341
  333.2 382.2 %reduce-scatter.3.cloned.1.call-start = ((), (), s32[]{:S(2)}) async-start(), calls=%async_computation.5 | async-start | bytes 10616832 | tf_op jit(solution)/shard_map/reduce_scatter | solution.py:638
  486.7 32.8 %collective-permute-start.15 = (f32[16,8,512]{2,1,0:T(8,128)S(1)}, f32[16,8,512]{2,1,0:T(8,128)S(1)}, u32[]{:S(2)}, u32[]{:S(2)}) collective-permute-start(f32[16,8,512]{2,1,0:T(8,128)S(1)} %shard_map.221.refs_0_), channel_id=1, source_target_pairs={{0,1},{1,0},{2,3},{3,2},{4,5},{5,4},{6,7},{7,6},{8,9},{9,8},{10,11... | collective-permute-start | bytes 786440 | tf_op jit(solution)/shard_map/ppermute | solution.py:341
  578.7 197.1 %all-reduce.8.cloned.1.call-start = ((), (), s32[]{:S(2)}) async-start(), calls=%async_computation.6 | async-start | bytes 2949120 | tf_op jit(solution)/shard_map/psum | solution.py:659
  607.3 89.8 %collective-permute-start.18 = (bf16[3,128,2048]{2,1,0:T(8,128)(2,1)}, bf16[3,128,2048]{2,1,0:T(8,128)(2,1)S(1)}, u32[]{:S(2)}, u32[]{:S(2)}) collective-permute-start(bf16[3,128,2048]{2,1,0:T(8,128)(2,1)} %get-tuple-element.155), channel_id=1, source_target_pairs={{0,1},{1,0},{2,3},{3,2},{4,5},{5,4},{6,7},{7,6},{8,9},{9,8},{10,11... | collective-permute-start | bytes 4718600 | tf_op jit(solution)/shard_map/ppermute | solution.py:341
  607.9 89.7 %collective-permute-start.19 = (bf16[3,128,2048]{2,1,0:T(8,128)(2,1)}, bf16[3,128,2048]{2,1,0:T(8,128)(2,1)S(1)}, u32[]{:S(2)}, u32[]{:S(2)}) collective-permute-start(bf16[3,128,2048]{2,1,0:T(8,128)(2,1)} %get-tuple-element.156), channel_id=1, source_target_pairs={{0,2},{1,3},{2,0},{3,1},{4,6},{5,7},{6,4},{7,5},{8,10},{9,11},{10,... | collective-permute-start | bytes 4718600 | tf_op jit(solution)/shard_map/ppermute | solution.py:341
  609.3 88.3 %collective-permute-start.20 = (bf16[3,128,2048]{2,1,0:T(8,128)(2,1)S(1)}, bf16[3,128,2048]{2,1,0:T(8,128)(2,1)S(1)}, u32[]{:S(2)}, u32[]{:S(2)}) collective-permute-start(bf16[3,128,2048]{2,1,0:T(8,128)(2,1)S(1)} %copy-done.2), channel_id=1, source_target_pairs={{0,3},{1,2},{2,1},{3,0},{4,7},{5,6},{6,5},{7,4},{8,11},{9,10},{10,... | collective-permute-start | bytes 4718600 | tf_op jit(solution)/shard_map/ppermute | solution.py:341
  613.0 123.5 %collective-permute-start.21 = (bf16[3,128,2048]{2,1,0:T(8,128)(2,1)}, bf16[3,128,2048]{2,1,0:T(8,128)(2,1)}, u32[]{:S(2)}, u32[]{:S(2)}) collective-permute-start(bf16[3,128,2048]{2,1,0:T(8,128)(2,1)} %get-tuple-element.164), channel_id=1, source_target_pairs={{0,1},{1,0},{2,3},{3,2},{4,5},{5,4},{6,7},{7,6},{8,9},{9,8},{10,11... | collective-permute-start | bytes 4718600 | tf_op jit(solution)/shard_map/ppermute | solution.py:341
  613.6 149.5 %collective-permute-start.23 = (bf16[3,128,2048]{2,1,0:T(8,128)(2,1)}, bf16[3,128,2048]{2,1,0:T(8,128)(2,1)}, u32[]{:S(2)}, u32[]{:S(2)}) collective-permute-start(bf16[3,128,2048]{2,1,0:T(8,128)(2,1)} %get-tuple-element.149.refs_2_), channel_id=1, source_target_pairs={{0,3},{1,2},{2,1},{3,0},{4,7},{5,6},{6,5},{7,4},{8,11},{9,10},{10,... | collective-permute-start | bytes 4718600 | tf_op jit(solution)/shard_map/ppermute | solution.py:341
  697.1 66.0 %collective-permute-start.22 = (bf16[3,128,2048]{2,1,0:T(8,128)(2,1)}, bf16[3,128,2048]{2,1,0:T(8,128)(2,1)}, u32[]{:S(2)}, u32[]{:S(2)}) collective-permute-start(bf16[3,128,2048]{2,1,0:T(8,128)(2,1)} %get-tuple-element.165), channel_id=1, source_target_pairs={{0,2},{1,3},{2,0},{3,1},{4,6},{5,7},{6,4},{7,5},{8,10},{9,11},{10,... | collective-permute-start | bytes 4718600 | tf_op jit(solution)/shard_map/ppermute | solution.py:341
  715.5 347.2 %reduce-scatter.5.cloned.1.call-start = ((), (), s32[]{:S(2)}) async-start(), calls=%async_computation.7 | async-start | bytes 10616832 | tf_op jit(solution)/shard_map/reduce_scatter | solution.py:687
  874.2 37.7 %collective-permute-start.25 = (bf16[3,128,2048]{2,1,0:T(8,128)(2,1)}, bf16[3,128,2048]{2,1,0:T(8,128)(2,1)}, u32[]{:S(2)}, u32[]{:S(2)}) collective-permute-start(bf16[3,128,2048]{2,1,0:T(8,128)(2,1)} %get-tuple-element.170), channel_id=1, source_target_pairs={{0,1},{1,0},{2,3},{3,2},{4,5},{5,4},{6,7},{7,6},{8,9},{9,8},{10,11... | collective-permute-start | bytes 4718600 | tf_op jit(solution)/shard_map/ppermute | solution.py:341
  874.3 68.2 %collective-permute-start.26 = (bf16[3,128,2048]{2,1,0:T(8,128)(2,1)}, bf16[3,128,2048]{2,1,0:T(8,128)(2,1)}, u32[]{:S(2)}, u32[]{:S(2)}) collective-permute-start(bf16[3,128,2048]{2,1,0:T(8,128)(2,1)} %get-tuple-element.171), channel_id=1, source_target_pairs={{0,2},{1,3},{2,0},{3,1},{4,6},{5,7},{6,4},{7,5},{8,10},{9,11},{10,... | collective-permute-start | bytes 4718600 | tf_op jit(solution)/shard_map/ppermute | solution.py:341
  877.4 65.8 %collective-permute-start.27 = (bf16[3,128,2048]{2,1,0:T(8,128)(2,1)}, bf16[3,128,2048]{2,1,0:T(8,128)(2,1)}, u32[]{:S(2)}, u32[]{:S(2)}) collective-permute-start(bf16[3,128,2048]{2,1,0:T(8,128)(2,1)} %get-tuple-element.172), channel_id=1, source_target_pairs={{0,3},{1,2},{2,1},{3,0},{4,7},{5,6},{6,5},{7,4},{8,11},{9,10},{10,... | collective-permute-start | bytes 4718600 | tf_op jit(solution)/shard_map/ppermute | solution.py:341
  952.2 98.2 %collective-permute-start.35 = (bf16[3,2048,128]{1,2,0:T(8,128)(2,1)}, bf16[3,2048,128]{1,2,0:T(8,128)(2,1)}, u32[]{:S(2)}, u32[]{:S(2)}) collective-permute-start(bf16[3,2048,128]{1,2,0:T(8,128)(2,1)} %get-tuple-element.252), channel_id=1, source_target_pairs={{0,0},{2,1},{4,2},{6,3},{8,4},{10,5},{12,6},{14,7},{16,8},{18,9},{... | collective-permute-start | bytes 4718600 | tf_op jit(solution)/shard_map/ppermute | solution.py:412
  954.6 95.9 %collective-permute-start.36 = (bf16[3,2048,128]{1,2,0:T(8,128)(2,1)S(1)}, bf16[3,2048,128]{1,2,0:T(8,128)(2,1)}, u32[]{:S(2)}, u32[]{:S(2)}) collective-permute-start(bf16[3,2048,128]{1,2,0:T(8,128)(2,1)S(1)} %select_bitcast_fusion), channel_id=1, source_target_pairs={{1,0},{3,1},{5,2},{7,3},{9,4},{11,5},{13,6},{15,7},{17,8},{19,9},{... | collective-permute-start | bytes 4718600 | tf_op jit(solution)/shard_map/ppermute | solution.py:413
  966.9 71.0 %collective-permute-start.34 = (f32[890,128]{1,0:T(8,128)S(1)}, f32[890,128]{1,0:T(8,128)S(1)}, u32[]{:S(2)}, u32[]{:S(2)}) collective-permute-start(f32[890,128]{1,0:T(8,128)S(1)} %get-tuple-element.286), channel_id=1, source_target_pairs={{0,3},{1,2},{2,1},{3,0},{4,7},{5,6},{6,5},{7,4},{8,11},{9,10},{10,... | collective-permute-start | bytes 1367048 | tf_op jit(solution)/shard_map/ppermute | solution.py:341
  970.5 75.7 %collective-permute-start.33 = (f32[890,128]{1,0:T(8,128)S(1)}, f32[890,128]{1,0:T(8,128)S(1)}, u32[]{:S(2)}, u32[]{:S(2)}) collective-permute-start(f32[890,128]{1,0:T(8,128)S(1)} %get-tuple-element.287), channel_id=1, source_target_pairs={{0,2},{1,3},{2,0},{3,1},{4,6},{5,7},{6,4},{7,5},{8,10},{9,11},{10,... | collective-permute-start | bytes 1367048 | tf_op jit(solution)/shard_map/ppermute | solution.py:341
  970.5 75.7 %collective-permute-start.32 = (f32[890,128]{1,0:T(8,128)S(1)}, f32[890,128]{1,0:T(8,128)S(1)}, u32[]{:S(2)}, u32[]{:S(2)}) collective-permute-start(f32[890,128]{1,0:T(8,128)S(1)} %get-tuple-element.285), channel_id=1, source_target_pairs={{0,1},{1,0},{2,3},{3,2},{4,5},{5,4},{6,7},{7,6},{8,9},{9,8},{10,11... | collective-permute-start | bytes 1367048 | tf_op jit(solution)/shard_map/ppermute | solution.py:341
  (97 other events, 1936.8 us)
Sparse Core Ops, SparseCore 0:
  144.2 96.2 all-gather.2
  242.1 89.1 all-gather.4
  334.3 66.8 all-reduce.5
  578.9 96.6 reduce-scatter.2
  715.6 60.2 all-reduce.7
  837.7 96.7 reduce-scatter.4
